TPU v7x, 32 devices: a whole 2x2x4 slice. The times are simulated.
32 devices in a mesh: blk: 8 (over z, y), col: 4 (over x, core).
Axes of the slice: x: 2, y: 2, z: 4, core: 2. Of those that a mesh axis runs over, the one named last changes fastest.
Arguments:
- amps: bfloat16 [8, 4, 2, 128, 128], P('blk', 'col'), may hold values from -6 to 6
- driver: float32 [8, 4, 2, 128, 128], P('blk', 'col')
- pattern: int32 [8, 4, 2, 8, 2], P('blk', 'col'), may hold values from -1 to 7, as said below
- domain: int32 [8, 4, 2], P('blk', 'col'), may hold values from 32 to 128
- virt_energy: float32 [8, 4, 2, 128], P('blk', 'col'), may hold values from 0.5 to 4
- pair_gap: float32 [8, 4, 2], P('blk', 'col'), may hold values from 0.5 to 2
- integrals: bfloat16 [8, 128, 128], P('col'), may hold values from -0.125 to 0.125
Outputs:
- new_amps: float32 [8, 4, 2, 128, 128], P('blk', 'col')
- resid_rms: float32 [], replicated
Inputs may be any that keep to these rules, and one draw needn't show every extreme that they name: `pattern`: about a third of the entries are -1; the others name integral tiles of all owners.
All inputs are finite; a program needn't handle non-finite values.
Results may differ from a plain program's by a relative error of at most 0.0003.
Values may be sent and summed in bfloat16 or wider, within the bound.
No kernel may reach another device: no remote copies, remote signals or barrier semaphores. Data moves between devices by JAX's collectives and lax.ppermute only.
A program may use at most 64 MiB of HBM per device.

v0:
```python
import jax
import jax.numpy as jnp
from jax import lax
from jax.sharding import PartitionSpec as P


def from_behind(block, axis, distance):
    devices = range(lax.axis_size(axis))
    route = [((i - distance) % len(devices), i) for i in devices]
    return lax.ppermute(block, axis, route)


def per_device(amps, driver, pattern, domain, virt_energy, pair_gap, integrals):
    width = amps.shape[-1]
    per_block = amps.shape[2]
    rows = jnp.arange(width, dtype=jnp.int32)
    edge = (rows[None, :] < domain[0, 0][:, None]).astype(jnp.float32)
    mask = edge[:, :, None] * edge[:, None, :]
    held = amps[0, 0] * mask.astype(jnp.bfloat16)
    links = pattern[0, 0].reshape(per_block, -1)
    table = lax.all_gather(integrals, "col", axis=0, tiled=True)

    def couple(total, piece, start):
        count = piece.shape[0]
        idx = lax.dynamic_slice_in_dim(links, start, count, 1)
        valid = (idx >= 0).astype(jnp.bfloat16)
        tiles = table[jnp.maximum(idx, 0)] * valid[:, :, None, None]
        return total + jnp.einsum("qab,pqbc->pac", piece, tiles, preferred_element_type=jnp.float32)

    zero_total = jnp.zeros((per_block, width, width), jnp.float32)
    cycle_size = lax.axis_size("blk")
    own_place = lax.axis_index("blk")

    def cycle_step(turn, carry):
        total, visit = carry
        source = (own_place - turn) % cycle_size
        total = couple(total, visit, source * per_block)
        visit = from_behind(visit, "blk", 1)
        return (total, visit)

    total, visit = lax.fori_loop(0, cycle_size - 1, cycle_step, (zero_total, held))
    last_source = (own_place - (cycle_size - 1)) % cycle_size
    coupled = couple(total, visit, last_source * per_block)
    resid = mask * (driver[0, 0] + coupled)
    energy = virt_energy[0, 0]
    denom = energy[:, :, None] + energy[:, None, :] + pair_gap[0, 0][:, None, None]
    new_amps = held.astype(jnp.float32) + resid / denom
    squares = lax.psum(jnp.sum(resid * resid), ("blk", "col"))
    entries = float(lax.axis_size("blk") * lax.axis_size("col") * per_block * width * width)
    resid_rms = jnp.sqrt(squares / entries)
    return (new_amps[None, None], resid_rms)


def solution(mesh):
    in_specs = (
        P("blk", "col", None, None, None),
        P("blk", "col", None, None, None),
        P("blk", "col", None, None, None),
        P("blk", "col", None),
        P("blk", "col", None, None),
        P("blk", "col", None),
        P("col", None, None),
    )
    out_specs = (P("blk", "col", None, None, None), P())
    return jax.shard_map(
        per_device, mesh=mesh, in_specs=in_specs, out_specs=out_specs, check_vma=False
    )
```

profile of v0, /device:TPU:0, one launch (start us, length us, event | category | flops | bytes accessed | tf_op | source)
XLA Modules:
  0.0 103.2 jit_solution(4623955459091487829)
XLA Ops:
  0.6 1.0 copy.24
  1.6 0.7 copy-done.4
  2.6 0.7 copy-done.2
  3.4 7.2 %all_gather.3 = bf16[8,128,128]{2,1,0:T(8,128)(2,1)S(1)} all-gather(bf16[2,128,128]{2,1,0:T(8,128)(2,1)S(1)} %copy-done.1), channel_id=1, replica_groups=mesh['blk'=8,'col'=4] {'col'}, dimensions={0}, use_global_device_ids=true | all-gather | bytes 327680 | tf_op jit(solution)/shard_map/all_gather | solution.py:21
  10.6 49.8 %while.18 = (s32[]{:T(128)}, f32[2,128,128]{1,2,0:T(8,128)S(1)}, bf16[2,128,128]{2,1,0:T(8,128)(2,1)S(1)}, s32[]{:T(128)}, s32[2,16]{1,0:T(2,128)S(1)}, /*index=...) while((s32[]{:T(128)}, f32[2,128,128]{1,2,0:T(8,128)S(1)}, ...), condition=%wide.region_1.2_spmd.clone, body=%wide.region_0.1_spmd.clone.sunk | while | flops 16909344 | bytes 1380822 | solution.py:41
  10.6 1.6 %collective-permute-start = (bf16[2,128,128]{2,1,0:T(8,128)(2,1)S(1)}, bf16[2,128,128]{2,1,0:T(8,128)(2,1)S(1)}, u32[]{:S(2)}, u32[]{:S(2)}) collective-permute-start(bf16[2,128,128]{2,1,0:T(8,128)(2,1)S(1)} %copy.39), channel_id=1, source_target_pairs={{28,0},{0,4},{4,8},{8,12},{12,16},{16,20},{20,24},{24,28},{29,1},{... | collective-permute-start | bytes 196616 | tf_op jit(solution)/shard_map/while/body/eval_jaxpr/ppermute | solution.py:10
  12.5 0.6 gather_fusion
  13.2 0.3 fusion.20
  13.4 4.4 %collective-permute-done = bf16[2,128,128]{2,1,0:T(8,128)(2,1)S(1)} collective-permute-done((bf16[2,128,128]{2,1,0:T(8,128)(2,1)S(1)}, bf16[2,128,128]{2,1,0:T(8,128)(2,1)S(1)}, u32[]{:S(2)}, u32[]{:S(2)}) %collective-permute-start) | collective-permute-done | bytes 65568 | tf_op jit(solution)/shard_map/while/body/eval_jaxpr/ppermute | solution.py:10
  18.2 0.6 gather_fusion
  18.9 0.3 fusion.20
  19.1 5.7 %collective-permute-done = bf16[2,128,128]{2,1,0:T(8,128)(2,1)S(1)} collective-permute-done((bf16[2,128,128]{2,1,0:T(8,128)(2,1)S(1)}, bf16[2,128,128]{2,1,0:T(8,128)(2,1)S(1)}, u32[]{:S(2)}, u32[]{:S(2)}) %collective-permute-start) | collective-permute-done | bytes 65568 | tf_op jit(solution)/shard_map/while/body/eval_jaxpr/ppermute | solution.py:10
  25.1 0.6 gather_fusion
  25.8 0.3 fusion.20
  26.1 5.7 %collective-permute-done = bf16[2,128,128]{2,1,0:T(8,128)(2,1)S(1)} collective-permute-done((bf16[2,128,128]{2,1,0:T(8,128)(2,1)S(1)}, bf16[2,128,128]{2,1,0:T(8,128)(2,1)S(1)}, u32[]{:S(2)}, u32[]{:S(2)}) %collective-permute-start) | collective-permute-done | bytes 65568 | tf_op jit(solution)/shard_map/while/body/eval_jaxpr/ppermute | solution.py:10
  32.1 0.6 gather_fusion
  32.8 0.3 fusion.20
  33.1 5.7 %collective-permute-done = bf16[2,128,128]{2,1,0:T(8,128)(2,1)S(1)} collective-permute-done((bf16[2,128,128]{2,1,0:T(8,128)(2,1)S(1)}, bf16[2,128,128]{2,1,0:T(8,128)(2,1)S(1)}, u32[]{:S(2)}, u32[]{:S(2)}) %collective-permute-start) | collective-permute-done | bytes 65568 | tf_op jit(solution)/shard_map/while/body/eval_jaxpr/ppermute | solution.py:10
  39.1 0.6 gather_fusion
  39.8 0.3 fusion.20
  40.0 5.7 %collective-permute-done = bf16[2,128,128]{2,1,0:T(8,128)(2,1)S(1)} collective-permute-done((bf16[2,128,128]{2,1,0:T(8,128)(2,1)S(1)}, bf16[2,128,128]{2,1,0:T(8,128)(2,1)S(1)}, u32[]{:S(2)}, u32[]{:S(2)}) %collective-permute-start) | collective-permute-done | bytes 65568 | tf_op jit(solution)/shard_map/while/body/eval_jaxpr/ppermute | solution.py:10
  46.0 0.6 gather_fusion
  46.7 0.3 fusion.20
  47.0 6.4 %collective-permute-done = bf16[2,128,128]{2,1,0:T(8,128)(2,1)S(1)} collective-permute-done((bf16[2,128,128]{2,1,0:T(8,128)(2,1)S(1)}, bf16[2,128,128]{2,1,0:T(8,128)(2,1)S(1)}, u32[]{:S(2)}, u32[]{:S(2)}) %collective-permute-start) | collective-permute-done | bytes 65568 | tf_op jit(solution)/shard_map/while/body/eval_jaxpr/ppermute | solution.py:10
  53.7 0.6 gather_fusion
  54.7 5.7 %collective-permute-done = bf16[2,128,128]{2,1,0:T(8,128)(2,1)S(1)} collective-permute-done((bf16[2,128,128]{2,1,0:T(8,128)(2,1)S(1)}, bf16[2,128,128]{2,1,0:T(8,128)(2,1)S(1)}, u32[]{:S(2)}, u32[]{:S(2)}) %collective-permute-start) | collective-permute-done | bytes 65568 | tf_op jit(solution)/shard_map/while/body/eval_jaxpr/ppermute | solution.py:10
  60.6 0.6 gather_fusion.1
  61.4 0.7 copy-done
  62.1 0.6 copy-done.3
  62.7 0.9 multiply_reduce_fusion
  63.6 0.8 copy.29
  64.3 37.1 %psum.7 = f32[]{:T(128)} all-reduce(f32[]{:T(128)} %get-tuple-element.217), channel_id=1, replica_groups=mesh['blk'=8,'col'=4] {'blk','col'}, use_global_device_ids=true, to_apply=%region_3.4 | all-reduce | flops 1 | bytes 8 | tf_op jit(solution)/shard_map/psum | solution.py:48
  (69 shorter events, 3.8 us)
Async XLA Ops:
  1.6 0.7 copy-start.4
  2.4 1.0 copy-start.1
  2.6 0.7 copy-start.2
  10.6 7.2 %collective-permute-start = (bf16[2,128,128]{2,1,0:T(8,128)(2,1)S(1)}, bf16[2,128,128]{2,1,0:T(8,128)(2,1)S(1)}, u32[]{:S(2)}, u32[]{:S(2)}) collective-permute-start(bf16[2,128,128]{2,1,0:T(8,128)(2,1)S(1)} %copy.39), channel_id=1, source_target_pairs={{28,0},{0,4},{4,8},{8,12},{12,16},{16,20},{20,24},{24,28},{29,1},{... | collective-permute-start | bytes 196616 | tf_op jit(solution)/shard_map/while/body/eval_jaxpr/ppermute | solution.py:10
  17.9 7.0 %collective-permute-start = (bf16[2,128,128]{2,1,0:T(8,128)(2,1)S(1)}, bf16[2,128,128]{2,1,0:T(8,128)(2,1)S(1)}, u32[]{:S(2)}, u32[]{:S(2)}) collective-permute-start(bf16[2,128,128]{2,1,0:T(8,128)(2,1)S(1)} %copy.39), channel_id=1, source_target_pairs={{28,0},{0,4},{4,8},{8,12},{12,16},{16,20},{20,24},{24,28},{29,1},{... | collective-permute-start | bytes 196616 | tf_op jit(solution)/shard_map/while/body/eval_jaxpr/ppermute | solution.py:10
  24.8 7.0 %collective-permute-start = (bf16[2,128,128]{2,1,0:T(8,128)(2,1)S(1)}, bf16[2,128,128]{2,1,0:T(8,128)(2,1)S(1)}, u32[]{:S(2)}, u32[]{:S(2)}) collective-permute-start(bf16[2,128,128]{2,1,0:T(8,128)(2,1)S(1)} %copy.39), channel_id=1, source_target_pairs={{28,0},{0,4},{4,8},{8,12},{12,16},{16,20},{20,24},{24,28},{29,1},{... | collective-permute-start | bytes 196616 | tf_op jit(solution)/shard_map/while/body/eval_jaxpr/ppermute | solution.py:10
  31.8 7.0 %collective-permute-start = (bf16[2,128,128]{2,1,0:T(8,128)(2,1)S(1)}, bf16[2,128,128]{2,1,0:T(8,128)(2,1)S(1)}, u32[]{:S(2)}, u32[]{:S(2)}) collective-permute-start(bf16[2,128,128]{2,1,0:T(8,128)(2,1)S(1)} %copy.39), channel_id=1, source_target_pairs={{28,0},{0,4},{4,8},{8,12},{12,16},{16,20},{20,24},{24,28},{29,1},{... | collective-permute-start | bytes 196616 | tf_op jit(solution)/shard_map/while/body/eval_jaxpr/ppermute | solution.py:10
  38.8 7.0 %collective-permute-start = (bf16[2,128,128]{2,1,0:T(8,128)(2,1)S(1)}, bf16[2,128,128]{2,1,0:T(8,128)(2,1)S(1)}, u32[]{:S(2)}, u32[]{:S(2)}) collective-permute-start(bf16[2,128,128]{2,1,0:T(8,128)(2,1)S(1)} %copy.39), channel_id=1, source_target_pairs={{28,0},{0,4},{4,8},{8,12},{12,16},{16,20},{20,24},{24,28},{29,1},{... | collective-permute-start | bytes 196616 | tf_op jit(solution)/shard_map/while/body/eval_jaxpr/ppermute | solution.py:10
  45.8 7.7 %collective-permute-start = (bf16[2,128,128]{2,1,0:T(8,128)(2,1)S(1)}, bf16[2,128,128]{2,1,0:T(8,128)(2,1)S(1)}, u32[]{:S(2)}, u32[]{:S(2)}) collective-permute-start(bf16[2,128,128]{2,1,0:T(8,128)(2,1)S(1)} %copy.39), channel_id=1, source_target_pairs={{28,0},{0,4},{4,8},{8,12},{12,16},{16,20},{20,24},{24,28},{29,1},{... | collective-permute-start | bytes 196616 | tf_op jit(solution)/shard_map/while/body/eval_jaxpr/ppermute | solution.py:10
  53.4 7.0 %collective-permute-start = (bf16[2,128,128]{2,1,0:T(8,128)(2,1)S(1)}, bf16[2,128,128]{2,1,0:T(8,128)(2,1)S(1)}, u32[]{:S(2)}, u32[]{:S(2)}) collective-permute-start(bf16[2,128,128]{2,1,0:T(8,128)(2,1)S(1)} %copy.39), channel_id=1, source_target_pairs={{28,0},{0,4},{4,8},{8,12},{12,16},{16,20},{20,24},{24,28},{29,1},{... | collective-permute-start | bytes 196616 | tf_op jit(solution)/shard_map/while/body/eval_jaxpr/ppermute | solution.py:10
  61.1 0.9 copy-start
  62.0 0.7 copy-start.3
  62.0 0.7 copy-start.5
where the time goes:
time: 104 us; the launch traced here: 103 us
  blocking collectives  44.2 us (42%)
  waiting for transfers between devices  39.4 us (38%)
  local copies, waits for them, and re-layouts  11 us (11%)
  matrix products  2.63 us (3%)
  between operations  2.54 us (2%)
  starting transfers between devices  1.6 us (2%)
  other arithmetic  1.43 us (1%)
    ppermute x7, waiting for transfers between devices, from_behind(): return lax.ppermute(block, axis, route)  39.4 us
    psum x1, blocking collectives, per_device(): squares = lax.psum(jnp.sum(resid * resid), ('blk', 'col'))  37.1 us
    all_gather x1, blocking collectives, per_device(): table = lax.all_gather(integrals, 'col', axis=0, tiled=True)  7.19 us
    gather x16, local copies, waits for them, and re-layouts, couple(): tiles = table[jnp.maximum(idx, 0)] * valid[:, :, None, None]  5.62 us
    unnamed x17, local copies, waits for them, and re-layouts  4.61 us
    dot_general x8, matrix products, couple(): jnp.einsum('qab,pqbc->pac', piece, tiles, preferred_element_type=jnp.floa...  2.63 us
  transfers between devices with their start and end apart: 7, of which 7 were waited for; matrix products, arithmetic and copies ran while one was open for 8% of the time, Pallas kernels for 0%

commit v1 on v0

v1 whole, which is shorter than its diff:
```python
import jax
import jax.numpy as jnp
from jax import lax
from jax.experimental import pallas as pl
from jax.experimental.pallas import tpu as pltpu
from jax.sharding import PartitionSpec as P

VMEM = pltpu.VMEM
SMEM = pltpu.SMEM


def edges(size, limit):
    rows = lax.broadcasted_iota(jnp.int32, (size, size), 0)
    cols = lax.broadcasted_iota(jnp.int32, (size, size), 1)
    return (rows < limit) & (cols < limit)


def hold_kernel(domain, amps, held):
    for p in range(amps.shape[0]):
        inside = edges(amps.shape[-1], domain[p])
        held[p] = jnp.where(inside, amps[p].astype(jnp.float32), 0.0).astype(held.dtype)


def couple_kernel(links, domain, gap, visits, table, driver, energy, energy_t, held, new, squares):
    pairs, width = held.shape[0], held.shape[-1]
    sources, per_source = visits.shape[0], visits.shape[1]
    acc = None

    def tile(p, t):
        k = links[p, t]
        block = table[jnp.maximum(k, 0)]
        return jnp.where(k >= 0, block, jnp.zeros_like(block))

    for s in range(sources):
        left = jnp.concatenate([visits[s, q] for q in range(per_source)], axis=1)
        right = jnp.concatenate(
            [
                jnp.concatenate([tile(p, s * per_source + q) for p in range(pairs)], axis=1)
                for q in range(per_source)
            ],
            axis=0,
        )
        part = jnp.dot(left, right, preferred_element_type=jnp.float32)
        acc = part if acc is None else acc + part
    total = jnp.zeros((1, width), jnp.float32)
    for p in range(pairs):
        inside = edges(width, domain[p])
        resid = jnp.where(inside, driver[p] + acc[:, p * width:(p + 1) * width], 0.0)
        denom = energy_t[:, p:p + 1] + energy[p:p + 1, :] + gap[p]
        new[p] = held[p].astype(jnp.float32) + resid / denom
        total = total + jnp.sum(resid * resid, axis=0, keepdims=True)
    squares[...] = jnp.broadcast_to(total, squares.shape)


def per_device(amps, driver, pattern, domain, virt_energy, pair_gap, integrals):
    pairs, width = amps.shape[2], amps.shape[-1]
    blocks, groups = lax.axis_size("blk"), lax.axis_size("col")
    links = pattern[0, 0].reshape(pairs, -1)
    spec = lambda space: pl.BlockSpec(memory_space=space)
    held = pl.pallas_call(
        hold_kernel,
        out_shape=jax.ShapeDtypeStruct((pairs, width, width), jnp.bfloat16),
        in_specs=[spec(SMEM), spec(VMEM)],
        out_specs=spec(VMEM),
    )(domain[0, 0], amps[0, 0])
    visits = lax.all_to_all(jnp.broadcast_to(held[None], (blocks,) + held.shape), "blk", 0, 0)
    table = lax.all_gather(integrals, "col", axis=0, tiled=True)
    energy = virt_energy[0, 0]
    new, squares = pl.pallas_call(
        couple_kernel,
        out_shape=[
            jax.ShapeDtypeStruct((pairs, width, width), jnp.float32),
            jax.ShapeDtypeStruct((blocks * groups, width), jnp.float32),
        ],
        in_specs=[spec(SMEM)] * 3 + [spec(VMEM)] * 6,
        out_specs=[spec(VMEM)] * 2,
    )(links, domain[0, 0], pair_gap[0, 0], visits, table, driver[0, 0], energy, energy.T, held)
    everyone = lax.all_to_all(squares, ("blk", "col"), 0, 0, tiled=True)
    entries = float(blocks * groups * pairs * width * width)
    resid_rms = jnp.sqrt(jnp.sum(everyone) / entries)
    return (new[None, None], resid_rms)


def solution(mesh):
    in_specs = (
        P("blk", "col", None, None, None),
        P("blk", "col", None, None, None),
        P("blk", "col", None, None, None),
        P("blk", "col", None),
        P("blk", "col", None, None),
        P("blk", "col", None),
        P("col", None, None),
    )
    out_specs = (P("blk", "col", None, None, None), P())
    return jax.shard_map(
        per_device, mesh=mesh, in_specs=in_specs, out_specs=out_specs, check_vma=False
    )
```

time: 104 us -> 42.4 us (0.41)
  waiting for transfers between devices: 39.4 us -> 6.66 us
  blocking collectives: 44.2 us -> 17 us
  local copies, waits for them, and re-layouts: 11 us -> 4.1 us
  starting transfers between devices: 1.6 us -> 7.41 us
  Pallas kernels: 0 us -> 3.7 us
  matrix products: 2.63 us -> 0 us
    ppermute x7 -> x0, waiting for transfers between devices: 39.4 us -> none  [from_behind(): return lax.ppermute(block, axis, route)]
    psum x1 -> x0, blocking collectives: 37.1 us -> none  [per_device(): squares = lax.psum(jnp.sum(resid * resid), ('blk', 'col'))]
    all_to_all x0 -> x1, blocking collectives: none -> 10.8 us  [per_device(): everyone = lax.all_to_all(squares, ('blk', 'col'), 0, 0, tiled=True)]
    all_to_all x0 -> x1, starting transfers between devices: none -> 7.41 us  [per_device(): lax.all_to_all(jnp.broadcast_to(held[None], (blocks,) + held.shape), 'blk...]
    all_to_all x0 -> x1, waiting for transfers between devices: none -> 6.66 us  [per_device(): lax.all_to_all(jnp.broadcast_to(held[None], (blocks,) + held.shape), 'blk...]
    gather x16 -> x0, local copies, waits for them, and re-layouts: 5.62 us -> none  [couple(): tiles = table[jnp.maximum(idx, 0)] * valid[:, :, None, None]]
    pallas_call x0 -> x2, Pallas kernels: none -> 3.7 us  [the longest x1 2.2 us: per_device(): pl.pallas_call(couple_kernel, out_shape=[jax.ShapeDtypeStruct((pairs, wid...]
    unnamed x17 -> x12, local copies, waits for them, and re-layouts: 4.61 us -> 1.04 us
  transfers between devices with their start and end apart: 7 -> 1, of which waited for: 7 -> 1; matrix products, arithmetic and copies ran while one was open for 8% -> 4% of each run, Pallas kernels for 0% -> 0%
where the time goes in v1:
time: 42.4 us; the launch traced here: 42 us
  blocking collectives  17 us (40%)
  starting transfers between devices  7.41 us (17%)
  waiting for transfers between devices  6.66 us (16%)
  local copies, waits for them, and re-layouts  4.1 us (10%)
  Pallas kernels  3.7 us (9%)
  between operations  2.48 us (6%)
  other arithmetic  0.63 us (1%)
    all_to_all x1, blocking collectives, per_device(): everyone = lax.all_to_all(squares, ('blk', 'col'), 0, 0, tiled=True)  10.8 us
    all_to_all x1, starting transfers between devices, per_device(): lax.all_to_all(jnp.broadcast_to(held[None], (blocks,) + held.shape), 'blk...  7.41 us
    all_to_all x1, waiting for transfers between devices, per_device(): lax.all_to_all(jnp.broadcast_to(held[None], (blocks,) + held.shape), 'blk...  6.66 us
    all_gather x1, blocking collectives, per_device(): table = lax.all_gather(integrals, 'col', axis=0, tiled=True)  6.22 us
    pallas_call x1, Pallas kernels, per_device(): pl.pallas_call(couple_kernel, out_shape=[jax.ShapeDtypeStruct((pairs, wid...  2.2 us
    broadcast_in_dim x1, local copies, waits for them, and re-layouts, per_device(): jnp.broadcast_to(held[None], (blocks,) + held.shape)  1.73 us
    pallas_call x1, Pallas kernels, per_device(): pl.pallas_call(hold_kernel, out_shape=jax.ShapeDtypeStruct((pairs, width,...  1.5 us
    unnamed x12, local copies, waits for them, and re-layouts  1.04 us
  transfers between devices with their start and end apart: 1, of which 1 were waited for; matrix products, arithmetic and copies ran while one was open for 4% of the time, Pallas kernels for 0%

profile of v1, /device:TPU:0, one launch (start us, length us, event | category | flops | bytes accessed | tf_op | source)
XLA Modules:
  0.0 42.0 jit_solution(2765712018976915123)
XLA Ops:
  0.6 1.5 %shard_map.86.held = bf16[2,128,128]{2,1,0:T(8,128)(2,1)} custom-call(s32[2]{0:T(128)} %bitcast.18, bf16[2,128,128]{2,1,0:T(8,128)(2,1)} %bitcast.16), custom_call_target="tpu_custom_call" | custom-call | tf_op jit(solution)/shard_map/pallas_call | solution.py:60
  2.1 1.7 %broadcast_in_dim.4 = bf16[8,2,128,128]{3,2,1,0:T(8,128)(2,1)} broadcast(bf16[2,128,128]{2,1,0:T(8,128)(2,1)} %shard_map.86.held), dimensions={1,2,3} | broadcast | bytes 589824 | tf_op jit(solution)/shard_map/broadcast_in_dim | solution.py:66
  3.9 0.0 copy-start.4
  3.9 7.4 %all-to-all-start = ((bf16[8,2,128,128]{3,2,1,0:T(8,128)(2,1)}), bf16[8,2,128,128]{3,2,1,0:T(8,128)(2,1)S(1)}, u32[]{:S(2)}, u32[]{:S(2)}) async-start(bf16[8,2,128,128]{3,2,1,0:T(8,128)(2,1)} %broadcast_in_dim.4), calls=%async_computation | async-start | bytes 1048576 | tf_op jit(solution)/shard_map/all_to_all | solution.py:66
  11.3 0.0 copy-done.4
  11.3 0.0 copy-start.2
  11.3 0.1 copy.16
  11.4 0.0 copy-start.1
  11.4 0.0 copy-start.3
  11.4 0.7 %copy.17.energy = f32[2,128]{1,0:T(2,128)} copy(f32[2,128]{0,1:T(8,128)S(1)} %bitcast.13) | data formatting | bytes 2048 | tf_op jit(solution)/shard_map/squeeze | solution.py:68
  12.1 0.0 copy-done.3
  12.1 0.1 copy.15
  12.2 0.7 %reshape_squeeze.3.links = s32[2,16]{1,0:T(2,128)} reshape(s32[1,1,2,8,2]{4,3,2,1,0:T(8,128)S(1)} %copy.15) | data formatting | bytes 256 | tf_op jit(solution)/shard_map/reshape;squeeze | solution.py:58
  12.9 0.0 copy-done.2
  12.9 6.2 %all_gather.3.table = bf16[8,128,128]{2,1,0:T(8,128)(2,1)} all-gather(bf16[2,128,128]{2,1,0:T(8,128)(2,1)S(1)} %copy-done.2), channel_id=1, replica_groups=mesh['blk'=8,'col'=4] {'col'}, dimensions={0}, use_global_device_ids=true | all-gather | bytes 327680 | tf_op jit(solution)/shard_map/all_gather | solution.py:67
  19.1 0.0 copy-done.1
  19.1 6.7 %all-to-all-done.visits = bf16[8,2,128,128]{3,2,1,0:T(8,128)(2,1)S(1)} async-done(((bf16[8,2,128,128]{3,2,1,0:T(8,128)(2,1)}), bf16[8,2,128,128]{3,2,1,0:T(8,128)(2,1)S(1)}, u32[]{:S(2)}, u32[]{:S(2)}) %all-to-all-start) | async-done | bytes 524320 | tf_op jit(solution)/shard_map/all_to_all | solution.py:66
  25.8 0.0 copy-start
  25.8 0.8 %copy-done = bf16[8,2,128,128]{3,2,1,0:T(8,128)(2,1)} copy-done((bf16[8,2,128,128]{3,2,1,0:T(8,128)(2,1)}, bf16[8,2,128,128]{3,2,1,0:T(8,128)(2,1)S(1)}, u32[]{:S(2)}) %copy-start) | copy-done | bytes 524312
  26.5 2.2 %shard_map.87 = (f32[2,128,128]{2,1,0:T(8,128)}, f32[32,128]{1,0:T(8,128)}) custom-call(s32[2,16]{1,0:T(2,128)} %reshape_squeeze.3.links, s32[2]{0:T(128)} %bitcast.19, f32[2]{0:T(128)} %bitcast.20, bf16[8,2,128,128]{3,2,1,0:T(8,128)(2,1)} %copy-done, bf16[8,128,128]{2,1,0:T(8,128)(2,1)} %all_gather.3.table, f32[2,128,128]{2,1,0:T(8,128)} %bitcast.15, ...), custom_call_target="tpu_custom_call" | custom-call | tf_op jit(solution)/shard_map/pallas_call | solution.py:69
  28.7 10.8 %all_to_all.14 = f32[32,1,128]{2,1,0:T(1,128)S(1)} all-to-all(f32[32,1,128]{2,1,0:T(1,128)} %bitcast.17), channel_id=1, replica_groups=mesh['blk'=8,'col'=4] {'blk','col'}, dimensions={0} | all-to-all | bytes 32768 | tf_op jit(solution)/shard_map/all_to_all | solution.py:78
  39.6 0.6 %reduce_sum.9 = f32[]{:T(128)} reduce(f32[32,1,128]{2,1,0:T(1,128)S(1)} %all_to_all.14, f32[]{:T(128)} %constant.1.clone.1), dimensions={0,1,2}, to_apply=%region_0.0 | reduce | flops 4095 | bytes 16392 | tf_op jit(solution)/shard_map/reduce_sum | solution.py:80
Async XLA Ops:
  3.9 7.4 %copy-start.4 = (f32[1,1,2,128]{3,2,1,0:T(2,128)S(1)}, f32[1,1,2,128]{3,2,1,0:T(2,128)}, u32[]{:S(2)}) copy-start(f32[1,1,2,128]{3,2,1,0:T(2,128)} %param.11) | copy-start | bytes 3076
  3.9 21.9 %all-to-all-start = ((bf16[8,2,128,128]{3,2,1,0:T(8,128)(2,1)}), bf16[8,2,128,128]{3,2,1,0:T(8,128)(2,1)S(1)}, u32[]{:S(2)}, u32[]{:S(2)}) async-start(bf16[8,2,128,128]{3,2,1,0:T(8,128)(2,1)} %broadcast_in_dim.4), calls=%async_computation | async-start | bytes 1048576 | tf_op jit(solution)/shard_map/all_to_all | solution.py:66
  11.3 1.6 %copy-start.2 = (bf16[2,128,128]{2,1,0:T(8,128)(2,1)S(1)}, bf16[2,128,128]{2,1,0:T(8,128)(2,1)}, u32[]{:S(2)}) copy-start(bf16[2,128,128]{2,1,0:T(8,128)(2,1)} %param.13) | copy-start | bytes 196612
  11.4 7.7 %copy-start.1 = (f32[1,1,2,128]{2,3,1,0:T(8,128)}, f32[1,1,2,128]{2,3,1,0:T(8,128)S(1)}, u32[]{:S(2)}) copy-start(f32[1,1,2,128]{2,3,1,0:T(8,128)S(1)} %copy.16) | copy-start | bytes 3076
  11.4 0.7 %copy-start.3 = (s32[1,1,2,8,2]{3,4,2,1,0:T(2,128)S(1)}, s32[1,1,2,8,2]{3,4,2,1,0:T(2,128)}, u32[]{:S(2)}) copy-start(s32[1,1,2,8,2]{3,4,2,1,0:T(2,128)} %param.9) | copy-start | bytes 388
  25.8 0.8 %copy-start = (bf16[8,2,128,128]{3,2,1,0:T(8,128)(2,1)}, bf16[8,2,128,128]{3,2,1,0:T(8,128)(2,1)S(1)}, u32[]{:S(2)}) copy-start(bf16[8,2,128,128]{3,2,1,0:T(8,128)(2,1)S(1)} %all-to-all-done.visits) | copy-start | bytes 1572868

commit v2 on v1

v2 whole, which is shorter than its diff:
```python
import functools

import jax
import jax.numpy as jnp
from jax import lax
from jax.experimental import pallas as pl
from jax.experimental.pallas import tpu as pltpu
from jax.sharding import PartitionSpec as P

HBM = pltpu.HBM
VMEM = pltpu.VMEM
SMEM = pltpu.SMEM
LIMIT = 8 << 20


def edges(size, limit):
    rows = lax.broadcasted_iota(jnp.int32, (size, size), 0)
    cols = lax.broadcasted_iota(jnp.int32, (size, size), 1)
    return (rows < limit) & (cols < limit)


def hold_kernel(domain_in, amps_in, held, domain, amps, sem):
    copies = [
        pltpu.make_async_copy(domain_in, domain, sem.at[0]),
        pltpu.make_async_copy(amps_in, amps, sem.at[1]),
    ]
    for copy in copies:
        copy.start()
    for copy in copies:
        copy.wait()
    for p in range(amps.shape[0]):
        inside = edges(amps.shape[-1], domain[p])
        held[p] = jnp.where(inside, amps[p].astype(jnp.float32), 0.0).astype(held.dtype)


def product(left, right):
    return jnp.dot(left, right, preferred_element_type=jnp.float32)


def visits_of(ref, j, pairs):
    return jnp.concatenate([ref[j * pairs + q] for q in range(pairs)], axis=1)


def early_kernel(voffs, loffs, toffs, place, ring, links_in, domain_in, gap_in, driver_in, energy_in, *rest):
    visits = rest[:len(voffs)]
    tables = rest[len(voffs):len(voffs) + len(toffs)]
    weights, base, mask, inverse = rest[len(voffs) + len(toffs):][:4]
    table, links, domain, gap, driver, energy, sem = rest[len(voffs) + len(toffs) + 4:]
    small = [
        pltpu.make_async_copy(src, dst, sem.at[i])
        for i, (src, dst) in enumerate(
            [(links_in, links), (domain_in, domain), (gap_in, gap), (driver_in, driver), (energy_in, energy)]
        )
    ]
    for copy in small:
        copy.start()
    pairs, width = base.shape[0], base.shape[-1]
    count = table.shape[0] - 1
    table[count] = jnp.zeros((width, width), table.dtype)
    for offs, ref in zip(toffs, tables):
        own = ref.shape[0] // len(offs)
        for j, off in enumerate(offs):
            table[pl.ds((ring[0] ^ off) * own, own)] = ref[j * own:(j + 1) * own]
    for copy in small:
        copy.wait()

    def tile(p, s, q):
        k = links[p, q, s]
        return table[jnp.where(k < 0, count, k)]

    def weight(off):
        src = place[0] ^ off
        return jnp.concatenate(
            [
                jnp.concatenate([tile(p, src, q) for p in range(pairs)], axis=1)
                for q in range(pairs)
            ],
            axis=0,
        )

    acc = None
    for offs, ref in zip(voffs, visits):
        for j, off in enumerate(offs):
            part = product(visits_of(ref, j, pairs), weight(off))
            acc = part if acc is None else acc + part
    for i, off in enumerate(loffs):
        weights[i] = weight(off)
    for p in range(pairs):
        inside = edges(width, domain[p])
        base[p] = jnp.where(inside, driver[p] + acc[:, p * width:(p + 1) * width], 0.0)
        mask[p] = inside.astype(jnp.float32)
        along = jnp.broadcast_to(energy[p:p + 1, :], (width, width))
        inverse[p] = 1.0 / (along.T + along + gap[p])


def late_kernel(counts, held, weights, base, mask, inverse, *rest):
    visits = rest[:len(counts)]
    new, squares = rest[len(counts):]
    pairs, width = base.shape[0], base.shape[-1]
    acc = None
    i = 0
    for n, ref in zip(counts, visits):
        for j in range(n):
            part = product(visits_of(ref, j, pairs), weights[i])
            acc = part if acc is None else acc + part
            i += 1
    total = jnp.zeros((1, width), jnp.float32)
    for p in range(pairs):
        resid = base[p] + mask[p] * acc[:, p * width:(p + 1) * width]
        new[p] = held[p].astype(jnp.float32) + resid * inverse[p]
        total = total + jnp.sum(resid * resid, axis=0, keepdims=True)
    squares[...] = jnp.broadcast_to(total, squares.shape)


def finish_kernel(entries, rows, out):
    total = jnp.sum(rows[...], axis=0, keepdims=True)
    total = jnp.sum(total, axis=1, keepdims=True)
    out[...] = jnp.sqrt(total / entries)


def xor(v, axis, k):
    return lax.ppermute(v, axis, [(i, i ^ k) for i in range(lax.axis_size(axis))])


def spread(own, axis, steps):
    have = {(0,): own}
    for k, pieces in steps:
        if pieces in have:
            v = have[pieces]
        else:
            v = jnp.concatenate([have[(i,)] for i in pieces], 0)
        have[tuple(i ^ k for i in pieces)] = xor(v, axis, k)
    return list(have.items())


def block_steps(size):
    far = list(range(size - 2, 2, -2))
    steps = [(k, (0,)) for k in far[1:]] + [(1, (0,))] + [(k, (0,)) for k in far[:1]]
    steps += [(2, (0, 1))] if size > 2 else []
    far.reverse()
    return steps + [(1, tuple(far[i:i + 2])) for i in range(0, len(far), 2)]


def tile_steps(size):
    far = tuple(range(2, size, 2))
    return [(k, (0,)) for k in far] + [(1, (0,) + far)]


def put(x, space):
    return pltpu.with_memory_space_constraint(x, space)


def spec(space):
    return pl.BlockSpec(memory_space=space)


def per_device(amps, driver, pattern, domain, virt_energy, pair_gap, integrals):
    pairs, width = amps.shape[2], amps.shape[-1]
    blocks, groups = lax.axis_size("blk"), lax.axis_size("col")
    count = groups * integrals.shape[0]
    links = pattern[0, 0].transpose(0, 2, 1)
    params = pltpu.CompilerParams(vmem_limit_bytes=LIMIT)
    DMA = pltpu.SemaphoreType.DMA
    tile = (pairs, width, width)
    held = pl.pallas_call(
        hold_kernel,
        out_shape=VMEM(tile, jnp.bfloat16),
        in_specs=[spec(HBM)] * 2,
        out_specs=spec(VMEM),
        scratch_shapes=[SMEM((pairs,), jnp.int32), VMEM(tile, jnp.bfloat16), DMA((2,))],
        compiler_params=params,
    )(put(domain[0, 0], HBM), put(amps[0, 0], HBM))
    pieces = spread(held, "blk", block_steps(blocks))
    tables = spread(integrals, "col", tile_steps(groups))
    early, late = pieces[:-1], pieces[-1:]
    place = lax.axis_index("blk").reshape(1)
    ring = lax.axis_index("col").reshape(1)
    loffs = [off for offs, _ in late for off in offs]
    args = [links, domain[0, 0], pair_gap[0, 0], driver[0, 0], virt_energy[0, 0]]
    big = [v for _, v in early] + [v for _, v in tables]
    weights, base, mask, inverse = pl.pallas_call(
        functools.partial(early_kernel, [o for o, _ in early], loffs, [o for o, _ in tables]),
        out_shape=[VMEM((len(loffs), pairs * width, pairs * width), jnp.bfloat16)] + [VMEM(tile, jnp.float32)] * 3,
        in_specs=[spec(SMEM)] * 2 + [spec(HBM)] * 5 + [spec(VMEM)] * len(big),
        out_specs=[spec(VMEM)] * 4,
        scratch_shapes=[
            VMEM((count + 1, width, width), jnp.bfloat16),
            SMEM(links.shape, jnp.int32),
            SMEM((pairs,), jnp.int32),
            SMEM((pairs,), jnp.float32),
            VMEM(tile, jnp.float32),
            VMEM((pairs, width), jnp.float32),
            DMA((5,)),
        ],
        compiler_params=params,
    )(place, ring, *[put(v, HBM) for v in args], *[put(v, VMEM) for v in big])
    new, squares = pl.pallas_call(
        functools.partial(late_kernel, [len(o) for o, _ in late]),
        out_shape=[
            VMEM(tile, jnp.float32),
            VMEM((blocks * groups, width), jnp.float32),
        ],
        in_specs=[spec(VMEM)] * (5 + len(late)),
        out_specs=[spec(VMEM)] * 2,
        compiler_params=params,
    )(*[put(v, VMEM) for v in (held, weights, base, mask, inverse)], *[put(v, VMEM) for _, v in late])
    entries = float(blocks * groups * pairs * width * width)
    rows = lax.all_to_all(squares, ("blk", "col"), 0, 0, tiled=True)
    rms = pl.pallas_call(
        functools.partial(finish_kernel, entries),
        out_shape=jax.ShapeDtypeStruct((1, 1), jnp.float32),
        in_specs=[spec(VMEM)],
        out_specs=spec(VMEM),
        compiler_params=params,
    )(put(rows, VMEM))
    return (new[None, None], rms.reshape(()))


def solution(mesh):
    in_specs = (
        P("blk", "col", None, None, None),
        P("blk", "col", None, None, None),
        P("blk", "col", None, None, None),
        P("blk", "col", None),
        P("blk", "col", None, None),
        P("blk", "col", None),
        P("col", None, None),
    )
    out_specs = (P("blk", "col", None, None, None), P())
    return jax.shard_map(
        per_device, mesh=mesh, in_specs=in_specs, out_specs=out_specs, check_vma=False
    )
```

time: 42.4 us -> 31.4 us (0.74)
  blocking collectives: 17 us -> 0 us
  waiting for transfers between devices: 6.66 us -> 13.2 us
  starting transfers between devices: 7.41 us -> 13.1 us
  local copies, waits for them, and re-layouts: 4.1 us -> 0.66 us
  between operations: 2.48 us -> 0.7 us
  other arithmetic: 0.63 us -> 0.04 us
    all_to_all x1 -> x0, blocking collectives: 10.8 us -> none  [per_device(): everyone = lax.all_to_all(squares, ('blk', 'col'), 0, 0, tiled=True)]
    ppermute x0 -> x7, starting transfers between devices: none -> 9.4 us  [xor(): lax.ppermute(v, axis, [(i, i ^ k) for i in range(lax.axis_size(axis))])]
    ppermute x0 -> x7, waiting for transfers between devices: none -> 6.67 us  [xor(): lax.ppermute(v, axis, [(i, i ^ k) for i in range(lax.axis_size(axis))])]
    all_gather x1 -> x0, blocking collectives: 6.22 us -> none  [per_device(): table = lax.all_gather(integrals, 'col', axis=0, tiled=True)]
    all_to_all x1, starting transfers between devices: 7.41 us -> 3.66 us  [per_device(): rows = lax.all_to_all(squares, ('blk', 'col'), 0, 0, tiled=True)]
    broadcast_in_dim x1 -> x0, local copies, waits for them, and re-layouts: 1.73 us -> none  [per_device(): jnp.broadcast_to(held[None], (blocks,) + held.shape)]
    another operation x1 -> x0, local copies, waits for them, and re-layouts: 0.67 us -> none  [per_device(): links = pattern[0, 0].reshape(pairs, -1)]
    squeeze x1 -> x0, local copies, waits for them, and re-layouts: 0.66 us -> none  [per_device(): energy = virt_energy[0, 0]]
  transfers between devices with their start and end apart: 1 -> 8, of which waited for: 1 -> 5; matrix products, arithmetic and copies ran while one was open for 4% -> 2% of each run, Pallas kernels for 0% -> 4%
where the time goes in v2:
time: 31.4 us; the launch traced here: 31.2 us
  waiting for transfers between devices  13.2 us (42%)
  starting transfers between devices  13.1 us (42%)
  Pallas kernels  3.61 us (11%)
  between operations  0.7 us (2%)
  local copies, waits for them, and re-layouts  0.66 us (2%)
    ppermute x7, starting transfers between devices, xor(): lax.ppermute(v, axis, [(i, i ^ k) for i in range(lax.axis_size(axis))])  9.4 us
    ppermute x7, waiting for transfers between devices, xor(): lax.ppermute(v, axis, [(i, i ^ k) for i in range(lax.axis_size(axis))])  6.67 us
    all_to_all x1, waiting for transfers between devices, per_device(): rows = lax.all_to_all(squares, ('blk', 'col'), 0, 0, tiled=True)  6.49 us
    all_to_all x1, starting transfers between devices, per_device(): rows = lax.all_to_all(squares, ('blk', 'col'), 0, 0, tiled=True)  3.66 us
    pallas_call x1, Pallas kernels, per_device(): pl.pallas_call(functools.partial(early_kernel, [o for o, _ in early], lof...  1.28 us
    pallas_call x1, Pallas kernels, per_device(): pl.pallas_call(hold_kernel, out_shape=VMEM(tile, jnp.bfloat16), in_specs=...  0.92 us
    pallas_call x1, Pallas kernels, per_device(): pl.pallas_call(functools.partial(late_kernel, [len(o) for o, _ in late]),...  0.81 us
    unnamed x3, local copies, waits for them, and re-layouts  0.66 us
  transfers between devices with their start and end apart: 8, of which 5 were waited for; matrix products, arithmetic and copies ran while one was open for 2% of the time, Pallas kernels for 4%

profile of v2, /device:TPU:0, one launch (start us, length us, event | category | flops | bytes accessed | tf_op | source)
XLA Modules:
  0.0 31.2 jit_solution(8475531735672459603)
XLA Ops:
  0.6 0.0 copy-start
  0.6 0.9 %shard_map.86.rest_0_.held = bf16[2,128,128]{2,1,0:T(8,128)(2,1)S(1)} custom-call(s32[2]{0:T(128)} %bitcast.21, bf16[2,128,128]{2,1,0:T(8,128)(2,1)} %bitcast.19), custom_call_target="tpu_custom_call" | custom-call | tf_op jit(solution)/shard_map/pallas_call | solution.py:165
  1.6 3.0 %collective-permute-start.1 = (bf16[2,128,128]{2,1,0:T(8,128)(2,1)S(1)}, bf16[2,128,128]{2,1,0:T(8,128)(2,1)S(1)}, u32[]{:S(2)}, u32[]{:S(2)}) collective-permute-start(bf16[2,128,128]{2,1,0:T(8,128)(2,1)S(1)} %shard_map.86.rest_0_.held), channel_id=1, source_target_pairs={{0,4},{4,0},{8,12},{12,8},{16,20},{20,16},{24,28},{28,24},{1,5},{5... | collective-permute-start | bytes 196616 | tf_op jit(solution)/shard_map/ppermute | solution.py:122
  4.6 2.6 %collective-permute-start = (bf16[2,128,128]{2,1,0:T(8,128)(2,1)S(1)}, bf16[2,128,128]{2,1,0:T(8,128)(2,1)S(1)}, u32[]{:S(2)}, u32[]{:S(2)}) collective-permute-start(bf16[2,128,128]{2,1,0:T(8,128)(2,1)S(1)} %shard_map.86.rest_0_.held), channel_id=1, source_target_pairs={{0,16},{4,20},{8,24},{12,28},{16,0},{20,4},{24,8},{28,12},{1,17},{... | collective-permute-start | bytes 196616 | tf_op jit(solution)/shard_map/ppermute | solution.py:122
  7.2 1.3 %collective-permute-start.2 = (bf16[2,128,128]{2,1,0:T(8,128)(2,1)S(1)}, bf16[2,128,128]{2,1,0:T(8,128)(2,1)S(1)}, u32[]{:S(2)}, u32[]{:S(2)}) collective-permute-start(bf16[2,128,128]{2,1,0:T(8,128)(2,1)S(1)} %shard_map.86.rest_0_.held), channel_id=1, source_target_pairs={{0,24},{4,28},{8,16},{12,20},{16,8},{20,12},{24,0},{28,4},{1,25},{... | collective-permute-start | bytes 196616 | tf_op jit(solution)/shard_map/ppermute | solution.py:122
  8.5 0.0 copy-done
  8.5 1.5 %collective-permute-start.4 = (bf16[2,128,128]{2,1,0:T(8,128)(2,1)S(1)}, bf16[2,128,128]{2,1,0:T(8,128)(2,1)S(1)}, u32[]{:S(2)}, u32[]{:S(2)}) collective-permute-start(bf16[2,128,128]{2,1,0:T(8,128)(2,1)S(1)} %copy-done), channel_id=1, source_target_pairs={{0,2},{1,3},{2,0},{3,1},{4,6},{5,7},{6,4},{7,5},{8,10},{9,11},{10,... | collective-permute-start | bytes 196616 | tf_op jit(solution)/shard_map/ppermute | solution.py:122
  10.0 0.0 collective-permute-done.1.rest_2_
  10.0 0.3 collective-permute-start.3
  10.3 2.5 %collective-permute-done.4.rest_6_ = bf16[2,128,128]{2,1,0:T(8,128)(2,1)S(1)} collective-permute-done((bf16[2,128,128]{2,1,0:T(8,128)(2,1)S(1)}, bf16[2,128,128]{2,1,0:T(8,128)(2,1)S(1)}, u32[]{:S(2)}, u32[]{:S(2)}) %collective-permute-start.4) | collective-permute-done | bytes 65568 | tf_op jit(solution)/shard_map/ppermute | solution.py:122
  12.8 0.1 collective-permute-start.5
  12.9 0.0 collective-permute-done.rest_1_
  12.9 1.0 %collective-permute-done.2.rest_3_ = bf16[2,128,128]{2,1,0:T(8,128)(2,1)S(1)} collective-permute-done((bf16[2,128,128]{2,1,0:T(8,128)(2,1)S(1)}, bf16[2,128,128]{2,1,0:T(8,128)(2,1)S(1)}, u32[]{:S(2)}, u32[]{:S(2)}) %collective-permute-start.2) | collective-permute-done | bytes 65568 | tf_op jit(solution)/shard_map/ppermute | solution.py:122
  14.0 0.6 %collective-permute-start.6 = (bf16[4,128,128]{2,1,0:T(8,128)(2,1)S(1)}, bf16[4,128,128]{2,1,0:T(8,128)(2,1)S(1)}, u32[]{:S(2)}, u32[]{:S(2)}) collective-permute-start(bf16[4,128,128]{2,1,0:T(8,128)(2,1)S(1)} %pad_maximum_fusion.2), channel_id=1, source_target_pairs={{0,4},{4,0},{8,12},{12,8},{16,20},{20,16},{24,28},{28,24},{1,5},{5... | collective-permute-start | bytes 393224 | tf_op jit(solution)/shard_map/ppermute | solution.py:122
  14.5 0.7 %collective-permute-done.3.rest_4_ = bf16[4,128,128]{2,1,0:T(8,128)(2,1)S(1)} collective-permute-done((bf16[4,128,128]{2,1,0:T(8,128)(2,1)S(1)}, bf16[4,128,128]{2,1,0:T(8,128)(2,1)S(1)}, u32[]{:S(2)}, u32[]{:S(2)}) %collective-permute-start.3) | collective-permute-done | bytes 131104 | tf_op jit(solution)/shard_map/ppermute | solution.py:122
  15.2 0.0 collective-permute-done.5.rest_7_
  15.2 1.3 %shard_map.87 = (bf16[2,256,256]{2,1,0:T(8,128)(2,1)S(1)}, f32[2,128,128]{2,1,0:T(8,128)S(1)}, f32[2,128,128]{2,1,0:T(8,128)S(1)}, f32[2,128,128]{2,1,0:T(8,128)S(1)}) custom-call(s32[1]{0:T(128)} %bitcast.2.place, s32[1]{0:T(128)} %bitcast.3.ring, s32[2,2,8]{2,1,0:T(2,128)} %bitcast.20, s32[2]{0:T(128)} %bitcast.22, f32[2]{0:T(128)} %bitcast.24, ...), custom_call_target="tpu_custom_call" | custom-call | tf_op jit(solution)/shard_map/pallas_call | solution.py:181
  16.5 2.5 %collective-permute-done.6.rest_0_ = bf16[4,128,128]{2,1,0:T(8,128)(2,1)S(1)} collective-permute-done((bf16[4,128,128]{2,1,0:T(8,128)(2,1)S(1)}, bf16[4,128,128]{2,1,0:T(8,128)(2,1)S(1)}, u32[]{:S(2)}, u32[]{:S(2)}) %collective-permute-start.6) | collective-permute-done | bytes 131104 | tf_op jit(solution)/shard_map/ppermute | solution.py:122
  19.0 0.8 %shard_map.88 = (f32[2,128,128]{2,1,0:T(8,128)S(1)}, f32[32,128]{1,0:T(8,128)}) custom-call(bf16[2,128,128]{2,1,0:T(8,128)(2,1)S(1)} %shard_map.86.rest_0_.held, bf16[2,256,256]{2,1,0:T(8,128)(2,1)S(1)} %get-tuple-element.8.weights, f32[2,128,128]{2,1,0:T(8,128)S(1)} %get-tuple-element.9.base, f32[2,128,128]{2,1,0:T(8,128)S(1)} %get-tuple-element.10.mask, ...), custom_call_target="tpu_custom_call" | custom-call | tf_op jit(solution)/shard_map/pallas_call | solution.py:197
  19.8 3.7 %all-to-all-start = ((f32[32,1,128]{2,1,0:T(1,128)}), f32[32,1,128]{2,1,0:T(1,128)S(1)}, u32[]{:S(2)}, u32[]{:S(2)}) async-start(f32[32,1,128]{2,1,0:T(1,128)} %bitcast.11), calls=%async_computation | async-start | bytes 32768 | tf_op jit(solution)/shard_map/all_to_all | solution.py:208
  23.5 0.7 %copy.10 = f32[1,1,2,128,128]{4,3,2,1,0:T(8,128)} copy(f32[1,1,2,128,128]{4,3,2,1,0:T(8,128)S(1)} %bitcast.16) | data formatting | bytes 262144
  24.1 6.5 %all-to-all-done = f32[32,1,128]{2,1,0:T(1,128)S(1)} async-done(((f32[32,1,128]{2,1,0:T(1,128)}), f32[32,1,128]{2,1,0:T(1,128)S(1)}, u32[]{:S(2)}, u32[]{:S(2)}) %all-to-all-start) | async-done | bytes 16416 | tf_op jit(solution)/shard_map/all_to_all | solution.py:208
  30.6 0.6 %shard_map.89 = f32[1,1]{1,0:T(1,128)} custom-call(f32[32,128]{1,0:T(8,128)S(1)} %bitcast.17), custom_call_target="tpu_custom_call" | custom-call | tf_op jit(solution)/shard_map/pallas_call | solution.py:209
  (3 shorter events, 0.0 us)
Async XLA Ops:
  0.6 7.9 %copy-start = (bf16[2,128,128]{2,1,0:T(8,128)(2,1)S(1)}, bf16[2,128,128]{2,1,0:T(8,128)(2,1)}, u32[]{:S(2)}) copy-start(bf16[2,128,128]{2,1,0:T(8,128)(2,1)} %rest_5_.1) | copy-start | bytes 196612
  1.6 8.5 %collective-permute-start.1 = (bf16[2,128,128]{2,1,0:T(8,128)(2,1)S(1)}, bf16[2,128,128]{2,1,0:T(8,128)(2,1)S(1)}, u32[]{:S(2)}, u32[]{:S(2)}) collective-permute-start(bf16[2,128,128]{2,1,0:T(8,128)(2,1)S(1)} %shard_map.86.rest_0_.held), channel_id=1, source_target_pairs={{0,4},{4,0},{8,12},{12,8},{16,20},{20,16},{24,28},{28,24},{1,5},{5... | collective-permute-start | bytes 196616 | tf_op jit(solution)/shard_map/ppermute | solution.py:122
  4.6 8.3 %collective-permute-start = (bf16[2,128,128]{2,1,0:T(8,128)(2,1)S(1)}, bf16[2,128,128]{2,1,0:T(8,128)(2,1)S(1)}, u32[]{:S(2)}, u32[]{:S(2)}) collective-permute-start(bf16[2,128,128]{2,1,0:T(8,128)(2,1)S(1)} %shard_map.86.rest_0_.held), channel_id=1, source_target_pairs={{0,16},{4,20},{8,24},{12,28},{16,0},{20,4},{24,8},{28,12},{1,17},{... | collective-permute-start | bytes 196616 | tf_op jit(solution)/shard_map/ppermute | solution.py:122
  7.2 6.8 %collective-permute-start.2 = (bf16[2,128,128]{2,1,0:T(8,128)(2,1)S(1)}, bf16[2,128,128]{2,1,0:T(8,128)(2,1)S(1)}, u32[]{:S(2)}, u32[]{:S(2)}) collective-permute-start(bf16[2,128,128]{2,1,0:T(8,128)(2,1)S(1)} %shard_map.86.rest_0_.held), channel_id=1, source_target_pairs={{0,24},{4,28},{8,16},{12,20},{16,8},{20,12},{24,0},{28,4},{1,25},{... | collective-permute-start | bytes 196616 | tf_op jit(solution)/shard_map/ppermute | solution.py:122
  8.5 4.3 %collective-permute-start.4 = (bf16[2,128,128]{2,1,0:T(8,128)(2,1)S(1)}, bf16[2,128,128]{2,1,0:T(8,128)(2,1)S(1)}, u32[]{:S(2)}, u32[]{:S(2)}) collective-permute-start(bf16[2,128,128]{2,1,0:T(8,128)(2,1)S(1)} %copy-done), channel_id=1, source_target_pairs={{0,2},{1,3},{2,0},{3,1},{4,6},{5,7},{6,4},{7,5},{8,10},{9,11},{10,... | collective-permute-start | bytes 196616 | tf_op jit(solution)/shard_map/ppermute | solution.py:122
  10.0 5.2 %collective-permute-start.3 = (bf16[4,128,128]{2,1,0:T(8,128)(2,1)S(1)}, bf16[4,128,128]{2,1,0:T(8,128)(2,1)S(1)}, u32[]{:S(2)}, u32[]{:S(2)}) collective-permute-start(bf16[4,128,128]{2,1,0:T(8,128)(2,1)S(1)} %pad_maximum_fusion), channel_id=1, source_target_pairs={{0,8},{4,12},{8,0},{12,4},{16,24},{20,28},{24,16},{28,20},{1,9},{5... | collective-permute-start | bytes 393224 | tf_op jit(solution)/shard_map/ppermute | solution.py:122
  12.8 2.4 %collective-permute-start.5 = (bf16[4,128,128]{2,1,0:T(8,128)(2,1)S(1)}, bf16[4,128,128]{2,1,0:T(8,128)(2,1)S(1)}, u32[]{:S(2)}, u32[]{:S(2)}) collective-permute-start(bf16[4,128,128]{2,1,0:T(8,128)(2,1)S(1)} %pad_maximum_fusion.1), channel_id=1, source_target_pairs={{0,1},{1,0},{2,3},{3,2},{4,5},{5,4},{6,7},{7,6},{8,9},{9,8},{10,11... | collective-permute-start | bytes 393224 | tf_op jit(solution)/shard_map/ppermute | solution.py:122
  14.0 5.0 %collective-permute-start.6 = (bf16[4,128,128]{2,1,0:T(8,128)(2,1)S(1)}, bf16[4,128,128]{2,1,0:T(8,128)(2,1)S(1)}, u32[]{:S(2)}, u32[]{:S(2)}) collective-permute-start(bf16[4,128,128]{2,1,0:T(8,128)(2,1)S(1)} %pad_maximum_fusion.2), channel_id=1, source_target_pairs={{0,4},{4,0},{8,12},{12,8},{16,20},{20,16},{24,28},{28,24},{1,5},{5... | collective-permute-start | bytes 393224 | tf_op jit(solution)/shard_map/ppermute | solution.py:122
  19.8 10.8 %all-to-all-start = ((f32[32,1,128]{2,1,0:T(1,128)}), f32[32,1,128]{2,1,0:T(1,128)S(1)}, u32[]{:S(2)}, u32[]{:S(2)}) async-start(f32[32,1,128]{2,1,0:T(1,128)} %bitcast.11), calls=%async_computation | async-start | bytes 32768 | tf_op jit(solution)/shard_map/all_to_all | solution.py:208

commit v3 on v2

--- a/solution.py
+++ b/solution.py
@@ -11,6 +11,7 @@
 VMEM = pltpu.VMEM
 SMEM = pltpu.SMEM
 LIMIT = 8 << 20
+NEWV = True
 
 
 def edges(size, limit):
@@ -41,7 +42,7 @@
     return jnp.concatenate([ref[j * pairs + q] for q in range(pairs)], axis=1)
 
 
-def early_kernel(voffs, loffs, toffs, place, ring, links_in, domain_in, gap_in, driver_in, energy_in, *rest):
+def early_kernel(voffs, loffs, toffs, place, ring, links_in, domain_in, gap_in, driver_in, energy_in, own_in, *rest):
     visits = rest[:len(voffs)]
     tables = rest[len(voffs):len(voffs) + len(toffs)]
     weights, base, mask, inverse = rest[len(voffs) + len(toffs):][:4]
@@ -52,13 +53,14 @@
             [(links_in, links), (domain_in, domain), (gap_in, gap), (driver_in, driver), (energy_in, energy)]
         )
     ]
+    pairs, width = base.shape[0], base.shape[-1]
+    count = table.shape[0] - 1
+    own = own_in.shape[0]
+    small.append(pltpu.make_async_copy(own_in, table.at[pl.ds(ring[0] * own, own)], sem.at[5]))
     for copy in small:
         copy.start()
-    pairs, width = base.shape[0], base.shape[-1]
-    count = table.shape[0] - 1
     table[count] = jnp.zeros((width, width), table.dtype)
     for offs, ref in zip(toffs, tables):
-        own = ref.shape[0] // len(offs)
         for j, off in enumerate(offs):
             table[pl.ds((ring[0] ^ off) * own, own)] = ref[j * own:(j + 1) * own]
     for copy in small:
@@ -84,7 +86,8 @@
             part = product(visits_of(ref, j, pairs), weight(off))
             acc = part if acc is None else acc + part
     for i, off in enumerate(loffs):
-        weights[i] = weight(off)
+        block = weight(off)
+        weights[i * block.shape[0]:(i + 1) * block.shape[0]] = block
     for p in range(pairs):
         inside = edges(width, domain[p])
         base[p] = jnp.where(inside, driver[p] + acc[:, p * width:(p + 1) * width], 0.0)
@@ -93,29 +96,24 @@
         inverse[p] = 1.0 / (along.T + along + gap[p])
 
 
-def late_kernel(counts, held, weights, base, mask, inverse, *rest):
-    visits = rest[:len(counts)]
-    new, squares = rest[len(counts):]
+def late_kernel(counts, weights, base, mask, *rest):
+    visits, (resid, squares) = rest[:len(counts)], rest[len(counts):]
     pairs, width = base.shape[0], base.shape[-1]
-    acc = None
-    i = 0
-    for n, ref in zip(counts, visits):
-        for j in range(n):
-            part = product(visits_of(ref, j, pairs), weights[i])
-            acc = part if acc is None else acc + part
-            i += 1
+    left = jnp.concatenate([visits_of(ref, j, pairs) for n, ref in zip(counts, visits) for j in range(n)], axis=1)
+    acc = product(left, weights[...])
     total = jnp.zeros((1, width), jnp.float32)
     for p in range(pairs):
-        resid = base[p] + mask[p] * acc[:, p * width:(p + 1) * width]
-        new[p] = held[p].astype(jnp.float32) + resid * inverse[p]
-        total = total + jnp.sum(resid * resid, axis=0, keepdims=True)
+        value = base[p] + mask[p] * acc[:, p * width:(p + 1) * width]
+        resid[p] = value
+        total = total + jnp.sum(value * value, axis=0, keepdims=True)
     squares[...] = jnp.broadcast_to(total, squares.shape)
 
 
-def finish_kernel(entries, rows, out):
+def finish_kernel(entries, rows, held, resid, inverse, new, rms):
+    new[...] = held[...].astype(jnp.float32) + resid[...] * inverse[...]
     total = jnp.sum(rows[...], axis=0, keepdims=True)
     total = jnp.sum(total, axis=1, keepdims=True)
-    out[...] = jnp.sqrt(total / entries)
+    rms[...] = jnp.sqrt(total / entries)
 
 
 def xor(v, axis, k):
@@ -123,13 +121,17 @@
 
 
 def spread(own, axis, steps):
-    have = {(0,): own}
+    have, single, n = {(0,): own}, {0: own}, own.shape[0]
     for k, pieces in steps:
         if pieces in have:
             v = have[pieces]
         else:
-            v = jnp.concatenate([have[(i,)] for i in pieces], 0)
-        have[tuple(i ^ k for i in pieces)] = xor(v, axis, k)
+            v = jnp.concatenate([single[i] for i in pieces], 0) if len(pieces) > 1 else single[pieces[0]]
+        got = xor(v, axis, k)
+        offs = tuple(i ^ k for i in pieces)
+        have[offs] = got
+        for j, i in enumerate(offs):
+            single[i] = got[j * n:(j + 1) * n] if len(offs) > 1 else got
     return list(have.items())
 
 
@@ -142,8 +144,8 @@
 
 
 def tile_steps(size):
-    far = tuple(range(2, size, 2))
-    return [(k, (0,)) for k in far] + [(1, (0,) + far)]
+    far = range(2, size, 2)
+    return [(k, (0,)) for k in far] + [(1, (0,))] + [(1, (k,)) for k in far]
 
 
 def put(x, space):
@@ -162,6 +164,7 @@
     params = pltpu.CompilerParams(vmem_limit_bytes=LIMIT)
     DMA = pltpu.SemaphoreType.DMA
     tile = (pairs, width, width)
+    tables = spread(integrals, "col", tile_steps(groups))
     held = pl.pallas_call(
         hold_kernel,
         out_shape=VMEM(tile, jnp.bfloat16),
@@ -171,17 +174,17 @@
         compiler_params=params,
     )(put(domain[0, 0], HBM), put(amps[0, 0], HBM))
     pieces = spread(held, "blk", block_steps(blocks))
-    tables = spread(integrals, "col", tile_steps(groups))
     early, late = pieces[:-1], pieces[-1:]
     place = lax.axis_index("blk").reshape(1)
     ring = lax.axis_index("col").reshape(1)
     loffs = [off for offs, _ in late for off in offs]
-    args = [links, domain[0, 0], pair_gap[0, 0], driver[0, 0], virt_energy[0, 0]]
+    args = [links, domain[0, 0], pair_gap[0, 0], driver[0, 0], virt_energy[0, 0], integrals]
+    tables = tables[1:]
     big = [v for _, v in early] + [v for _, v in tables]
     weights, base, mask, inverse = pl.pallas_call(
         functools.partial(early_kernel, [o for o, _ in early], loffs, [o for o, _ in tables]),
-        out_shape=[VMEM((len(loffs), pairs * width, pairs * width), jnp.bfloat16)] + [VMEM(tile, jnp.float32)] * 3,
-        in_specs=[spec(SMEM)] * 2 + [spec(HBM)] * 5 + [spec(VMEM)] * len(big),
+        out_shape=[VMEM((len(loffs) * pairs * width, pairs * width), jnp.bfloat16)] + [VMEM(tile, jnp.float32)] * 3,
+        in_specs=[spec(SMEM)] * 2 + [spec(HBM)] * 6 + [spec(VMEM)] * len(big),
         out_specs=[spec(VMEM)] * 4,
         scratch_shapes=[
             VMEM((count + 1, width, width), jnp.bfloat16),
@@ -190,29 +193,26 @@
             SMEM((pairs,), jnp.float32),
             VMEM(tile, jnp.float32),
             VMEM((pairs, width), jnp.float32),
-            DMA((5,)),
+            DMA((6,)),
         ],
         compiler_params=params,
     )(place, ring, *[put(v, HBM) for v in args], *[put(v, VMEM) for v in big])
-    new, squares = pl.pallas_call(
+    resid, squares = pl.pallas_call(
         functools.partial(late_kernel, [len(o) for o, _ in late]),
-        out_shape=[
-            VMEM(tile, jnp.float32),
-            VMEM((blocks * groups, width), jnp.float32),
-        ],
-        in_specs=[spec(VMEM)] * (5 + len(late)),
+        out_shape=[VMEM(tile, jnp.float32), VMEM((blocks * groups, width), jnp.float32)],
+        in_specs=[spec(VMEM)] * (3 + len(late)),
         out_specs=[spec(VMEM)] * 2,
         compiler_params=params,
-    )(*[put(v, VMEM) for v in (held, weights, base, mask, inverse)], *[put(v, VMEM) for _, v in late])
+    )(*[put(v, VMEM) for v in (weights, base, mask)], *[put(v, VMEM) for _, v in late])
     entries = float(blocks * groups * pairs * width * width)
     rows = lax.all_to_all(squares, ("blk", "col"), 0, 0, tiled=True)
-    rms = pl.pallas_call(
+    new, rms = pl.pallas_call(
         functools.partial(finish_kernel, entries),
-        out_shape=jax.ShapeDtypeStruct((1, 1), jnp.float32),
-        in_specs=[spec(VMEM)],
-        out_specs=spec(VMEM),
-        compiler_params=params,
-    )(put(rows, VMEM))
+        out_shape=[jax.ShapeDtypeStruct(tile, jnp.float32), jax.ShapeDtypeStruct((1, 1), jnp.float32)],
+        in_specs=[spec(VMEM)] * 4,
+        out_specs=[spec(VMEM)] * 2,
+        compiler_params=params,
+    )(*[put(v, VMEM) for v in (rows, held, resid, inverse)])
     return (new[None, None], rms.reshape(()))
 
 

time: 31.4 us -> 30.4 us (0.968)
  blocking collectives: 0 us -> 10.3 us
  waiting for transfers between devices: 13.2 us -> 6.24 us
  starting transfers between devices: 13.1 us -> 9.84 us
  local copies, waits for them, and re-layouts: 0.66 us -> 0.01 us
  Pallas kernels: 3.61 us -> 3.1 us
    all_to_all x0 -> x1, blocking collectives: none -> 10.3 us  [per_device(): rows = lax.all_to_all(squares, ('blk', 'col'), 0, 0, tiled=True)]
    all_to_all x1 -> x0, waiting for transfers between devices: 6.49 us -> none  [per_device(): rows = lax.all_to_all(squares, ('blk', 'col'), 0, 0, tiled=True)]
    all_to_all x1 -> x0, starting transfers between devices: 3.66 us -> none  [per_device(): rows = lax.all_to_all(squares, ('blk', 'col'), 0, 0, tiled=True)]
    unnamed x3 -> x2, local copies, waits for them, and re-layouts: 0.66 us -> 0.01 us
    pallas_call x1, Pallas kernels: 0.81 us -> 0.2 us  [per_device(): pl.pallas_call(functools.partial(late_kernel, [len(o) for o, _ in late]),...]
    ppermute x7 -> x8, starting transfers between devices: 9.4 us -> 9.84 us  [xor(): lax.ppermute(v, axis, [(i, i ^ k) for i in range(lax.axis_size(axis))])]
    ppermute x7 -> x8, waiting for transfers between devices: 6.67 us -> 6.24 us  [xor(): lax.ppermute(v, axis, [(i, i ^ k) for i in range(lax.axis_size(axis))])]
  transfers between devices with their start and end apart: 8 -> 8, of which waited for: 5 -> 4; matrix products, arithmetic and copies ran while one was open for 2% -> 0% of each run, Pallas kernels for 4% -> 4%
where the time goes in v3:
time: 30.4 us; the launch traced here: 30.2 us
  blocking collectives  10.3 us (34%)
  starting transfers between devices  9.84 us (32%)
  waiting for transfers between devices  6.24 us (21%)
  Pallas kernels  3.1 us (10%)
  between operations  0.68 us (2%)
    all_to_all x1, blocking collectives, per_device(): rows = lax.all_to_all(squares, ('blk', 'col'), 0, 0, tiled=True)  10.3 us
    ppermute x8, starting transfers between devices, xor(): lax.ppermute(v, axis, [(i, i ^ k) for i in range(lax.axis_size(axis))])  9.84 us
    ppermute x8, waiting for transfers between devices, xor(): lax.ppermute(v, axis, [(i, i ^ k) for i in range(lax.axis_size(axis))])  6.24 us
    pallas_call x1, Pallas kernels, per_device(): pl.pallas_call(functools.partial(early_kernel, [o for o, _ in early], lof...  1.3 us
    pallas_call x1, Pallas kernels, per_device(): pl.pallas_call(hold_kernel, out_shape=VMEM(tile, jnp.bfloat16), in_specs=...  0.92 us
    pallas_call x1, Pallas kernels, per_device(): pl.pallas_call(functools.partial(finish_kernel, entries), out_shape=[jax....  0.68 us
  transfers between devices with their start and end apart: 8, of which 4 were waited for; matrix products, arithmetic and copies ran while one was open for 0% of the time, Pallas kernels for 4%

profile of v3, /device:TPU:0, one launch (start us, length us, event | category | flops | bytes accessed | tf_op | source)
XLA Modules:
  0.0 30.2 jit_solution(1117255555400348300)
XLA Ops:
  0.6 0.0 copy-start
  0.6 0.9 %shard_map.86.rest_0_.held = bf16[2,128,128]{2,1,0:T(8,128)(2,1)S(1)} custom-call(s32[2]{0:T(128)} %bitcast.21, bf16[2,128,128]{2,1,0:T(8,128)(2,1)} %bitcast.19), custom_call_target="tpu_custom_call" | custom-call | tf_op jit(solution)/shard_map/pallas_call | solution.py:168
  1.6 3.0 %collective-permute-start.1 = (bf16[2,128,128]{2,1,0:T(8,128)(2,1)S(1)}, bf16[2,128,128]{2,1,0:T(8,128)(2,1)S(1)}, u32[]{:S(2)}, u32[]{:S(2)}) collective-permute-start(bf16[2,128,128]{2,1,0:T(8,128)(2,1)S(1)} %shard_map.86.rest_0_.held), channel_id=1, source_target_pairs={{0,4},{4,0},{8,12},{12,8},{16,20},{20,16},{24,28},{28,24},{1,5},{5... | collective-permute-start | bytes 196616 | tf_op jit(solution)/shard_map/ppermute | solution.py:120
  4.6 2.6 %collective-permute-start = (bf16[2,128,128]{2,1,0:T(8,128)(2,1)S(1)}, bf16[2,128,128]{2,1,0:T(8,128)(2,1)S(1)}, u32[]{:S(2)}, u32[]{:S(2)}) collective-permute-start(bf16[2,128,128]{2,1,0:T(8,128)(2,1)S(1)} %shard_map.86.rest_0_.held), channel_id=1, source_target_pairs={{0,16},{4,20},{8,24},{12,28},{16,0},{20,4},{24,8},{28,12},{1,17},{... | collective-permute-start | bytes 196616 | tf_op jit(solution)/shard_map/ppermute | solution.py:120
  7.2 1.3 %collective-permute-start.2 = (bf16[2,128,128]{2,1,0:T(8,128)(2,1)S(1)}, bf16[2,128,128]{2,1,0:T(8,128)(2,1)S(1)}, u32[]{:S(2)}, u32[]{:S(2)}) collective-permute-start(bf16[2,128,128]{2,1,0:T(8,128)(2,1)S(1)} %shard_map.86.rest_0_.held), channel_id=1, source_target_pairs={{0,24},{4,28},{8,16},{12,20},{16,8},{20,12},{24,0},{28,4},{1,25},{... | collective-permute-start | bytes 196616 | tf_op jit(solution)/shard_map/ppermute | solution.py:120
  8.5 0.0 copy-done
  8.5 1.5 %collective-permute-start.4 = (bf16[2,128,128]{2,1,0:T(8,128)(2,1)S(1)}, bf16[2,128,128]{2,1,0:T(8,128)(2,1)S(1)}, u32[]{:S(2)}, u32[]{:S(2)}) collective-permute-start(bf16[2,128,128]{2,1,0:T(8,128)(2,1)S(1)} %copy-done), channel_id=1, source_target_pairs={{0,2},{1,3},{2,0},{3,1},{4,6},{5,7},{6,4},{7,5},{8,10},{9,11},{10,... | collective-permute-start | bytes 196616 | tf_op jit(solution)/shard_map/ppermute | solution.py:120
  10.0 0.0 collective-permute-done.1.rest_2_
  10.1 0.3 collective-permute-start.3
  10.3 0.0 collective-permute-done.rest_1_
  10.3 3.6 %collective-permute-done.2.rest_3_ = bf16[2,128,128]{2,1,0:T(8,128)(2,1)S(1)} collective-permute-done((bf16[2,128,128]{2,1,0:T(8,128)(2,1)S(1)}, bf16[2,128,128]{2,1,0:T(8,128)(2,1)S(1)}, u32[]{:S(2)}, u32[]{:S(2)}) %collective-permute-start.2) | collective-permute-done | bytes 65568 | tf_op jit(solution)/shard_map/ppermute | solution.py:120
  14.0 0.6 %collective-permute-start.7 = (bf16[4,128,128]{2,1,0:T(8,128)(2,1)S(1)}, bf16[4,128,128]{2,1,0:T(8,128)(2,1)S(1)}, u32[]{:S(2)}, u32[]{:S(2)}) collective-permute-start(bf16[4,128,128]{2,1,0:T(8,128)(2,1)S(1)} %pad_maximum_fusion.1), channel_id=1, source_target_pairs={{0,4},{4,0},{8,12},{12,8},{16,20},{20,16},{24,28},{28,24},{1,5},{5... | collective-permute-start | bytes 393224 | tf_op jit(solution)/shard_map/ppermute | solution.py:120
  14.5 0.0 collective-permute-start.5
  14.5 0.0 collective-permute-done.4.rest_5_
  14.5 0.5 %collective-permute-start.6 = (bf16[2,128,128]{2,1,0:T(8,128)(2,1)S(1)}, bf16[2,128,128]{2,1,0:T(8,128)(2,1)S(1)}, u32[]{:S(2)}, u32[]{:S(2)}) collective-permute-start(bf16[2,128,128]{2,1,0:T(8,128)(2,1)S(1)} %collective-permute-done.4.rest_5_), channel_id=1, source_target_pairs={{0,1},{1,0},{2,3},{3,2},{4,5},{5,4},{6,7},{7,6},{8,9},{9,8},{10,11... | collective-permute-start | bytes 196616 | tf_op jit(solution)/shard_map/ppermute | solution.py:120
  15.1 0.7 %collective-permute-done.5.rest_6_ = bf16[2,128,128]{2,1,0:T(8,128)(2,1)S(1)} collective-permute-done((bf16[2,128,128]{2,1,0:T(8,128)(2,1)S(1)}, bf16[2,128,128]{2,1,0:T(8,128)(2,1)S(1)}, u32[]{:S(2)}, u32[]{:S(2)}) %collective-permute-start.5) | collective-permute-done | bytes 65568 | tf_op jit(solution)/shard_map/ppermute | solution.py:120
  15.8 0.2 collective-permute-done.6.rest_7_
  16.0 0.0 collective-permute-done.3.rest_4_
  16.0 1.3 %shard_map.87 = (bf16[512,256]{1,0:T(8,128)(2,1)S(1)}, f32[2,128,128]{2,1,0:T(8,128)S(1)}, f32[2,128,128]{2,1,0:T(8,128)S(1)}, f32[2,128,128]{2,1,0:T(8,128)S(1)}) custom-call(s32[1]{0:T(128)} %bitcast.place, s32[1]{0:T(128)} %bitcast.1.ring, s32[2,2,8]{2,1,0:T(2,128)} %bitcast.20, s32[2]{0:T(128)} %bitcast.22, f32[2]{0:T(128)} %bitcast.24, ...), custom_call_target="tpu_custom_call" | custom-call | tf_op jit(solution)/shard_map/pallas_call | solution.py:184
  17.3 1.7 %collective-permute-done.7.rest_0_ = bf16[4,128,128]{2,1,0:T(8,128)(2,1)S(1)} collective-permute-done((bf16[4,128,128]{2,1,0:T(8,128)(2,1)S(1)}, bf16[4,128,128]{2,1,0:T(8,128)(2,1)S(1)}, u32[]{:S(2)}, u32[]{:S(2)}) %collective-permute-start.7) | collective-permute-done | bytes 131104 | tf_op jit(solution)/shard_map/ppermute | solution.py:120
  19.0 0.2 shard_map.88
  19.2 10.3 %all_to_all.11 = f32[32,1,128]{2,1,0:T(1,128)S(1)} all-to-all(f32[32,1,128]{2,1,0:T(1,128)S(1)} %bitcast.17), channel_id=1, replica_groups=mesh['blk'=8,'col'=4] {'blk','col'}, dimensions={0} | all-to-all | bytes 32768 | tf_op jit(solution)/shard_map/all_to_all | solution.py:208
  29.5 0.7 %shard_map.89 = (f32[2,128,128]{2,1,0:T(8,128)}, f32[1,1]{1,0:T(1,128)}) custom-call(f32[32,128]{1,0:T(8,128)S(1)} %bitcast.16, bf16[2,128,128]{2,1,0:T(8,128)(2,1)S(1)} %shard_map.86.rest_0_.held, f32[2,128,128]{2,1,0:T(8,128)S(1)} %get-tuple-element.14.resid, f32[2,128,128]{2,1,0:T(8,128)S(1)} %get-tuple-element.15.inverse), custom_call_target="tpu_custom_call" | custom-call | tf_op jit(solution)/shard_map/pallas_call | solution.py:209
  (2 shorter events, 0.0 us)
Async XLA Ops:
  0.6 7.9 %copy-start = (bf16[2,128,128]{2,1,0:T(8,128)(2,1)S(1)}, bf16[2,128,128]{2,1,0:T(8,128)(2,1)}, u32[]{:S(2)}) copy-start(bf16[2,128,128]{2,1,0:T(8,128)(2,1)} %own_in.1) | copy-start | bytes 196612
  1.6 8.5 %collective-permute-start.1 = (bf16[2,128,128]{2,1,0:T(8,128)(2,1)S(1)}, bf16[2,128,128]{2,1,0:T(8,128)(2,1)S(1)}, u32[]{:S(2)}, u32[]{:S(2)}) collective-permute-start(bf16[2,128,128]{2,1,0:T(8,128)(2,1)S(1)} %shard_map.86.rest_0_.held), channel_id=1, source_target_pairs={{0,4},{4,0},{8,12},{12,8},{16,20},{20,16},{24,28},{28,24},{1,5},{5... | collective-permute-start | bytes 196616 | tf_op jit(solution)/shard_map/ppermute | solution.py:120
  4.6 5.8 %collective-permute-start = (bf16[2,128,128]{2,1,0:T(8,128)(2,1)S(1)}, bf16[2,128,128]{2,1,0:T(8,128)(2,1)S(1)}, u32[]{:S(2)}, u32[]{:S(2)}) collective-permute-start(bf16[2,128,128]{2,1,0:T(8,128)(2,1)S(1)} %shard_map.86.rest_0_.held), channel_id=1, source_target_pairs={{0,16},{4,20},{8,24},{12,28},{16,0},{20,4},{24,8},{28,12},{1,17},{... | collective-permute-start | bytes 196616 | tf_op jit(solution)/shard_map/ppermute | solution.py:120
  7.2 6.8 %collective-permute-start.2 = (bf16[2,128,128]{2,1,0:T(8,128)(2,1)S(1)}, bf16[2,128,128]{2,1,0:T(8,128)(2,1)S(1)}, u32[]{:S(2)}, u32[]{:S(2)}) collective-permute-start(bf16[2,128,128]{2,1,0:T(8,128)(2,1)S(1)} %shard_map.86.rest_0_.held), channel_id=1, source_target_pairs={{0,24},{4,28},{8,16},{12,20},{16,8},{20,12},{24,0},{28,4},{1,25},{... | collective-permute-start | bytes 196616 | tf_op jit(solution)/shard_map/ppermute | solution.py:120
  8.5 6.0 %collective-permute-start.4 = (bf16[2,128,128]{2,1,0:T(8,128)(2,1)S(1)}, bf16[2,128,128]{2,1,0:T(8,128)(2,1)S(1)}, u32[]{:S(2)}, u32[]{:S(2)}) collective-permute-start(bf16[2,128,128]{2,1,0:T(8,128)(2,1)S(1)} %copy-done), channel_id=1, source_target_pairs={{0,2},{1,3},{2,0},{3,1},{4,6},{5,7},{6,4},{7,5},{8,10},{9,11},{10,... | collective-permute-start | bytes 196616 | tf_op jit(solution)/shard_map/ppermute | solution.py:120
  10.1 5.9 %collective-permute-start.3 = (bf16[4,128,128]{2,1,0:T(8,128)(2,1)S(1)}, bf16[4,128,128]{2,1,0:T(8,128)(2,1)S(1)}, u32[]{:S(2)}, u32[]{:S(2)}) collective-permute-start(bf16[4,128,128]{2,1,0:T(8,128)(2,1)S(1)} %pad_maximum_fusion), channel_id=1, source_target_pairs={{0,8},{4,12},{8,0},{12,4},{16,24},{20,28},{24,16},{28,20},{1,9},{5... | collective-permute-start | bytes 393224 | tf_op jit(solution)/shard_map/ppermute | solution.py:120
  14.0 5.0 %collective-permute-start.7 = (bf16[4,128,128]{2,1,0:T(8,128)(2,1)S(1)}, bf16[4,128,128]{2,1,0:T(8,128)(2,1)S(1)}, u32[]{:S(2)}, u32[]{:S(2)}) collective-permute-start(bf16[4,128,128]{2,1,0:T(8,128)(2,1)S(1)} %pad_maximum_fusion.1), channel_id=1, source_target_pairs={{0,4},{4,0},{8,12},{12,8},{16,20},{20,16},{24,28},{28,24},{1,5},{5... | collective-permute-start | bytes 393224 | tf_op jit(solution)/shard_map/ppermute | solution.py:120
  14.5 1.3 %collective-permute-start.5 = (bf16[2,128,128]{2,1,0:T(8,128)(2,1)S(1)}, bf16[2,128,128]{2,1,0:T(8,128)(2,1)S(1)}, u32[]{:S(2)}, u32[]{:S(2)}) collective-permute-start(bf16[2,128,128]{2,1,0:T(8,128)(2,1)S(1)} %copy-done), channel_id=1, source_target_pairs={{0,1},{1,0},{2,3},{3,2},{4,5},{5,4},{6,7},{7,6},{8,9},{9,8},{10,11... | collective-permute-start | bytes 196616 | tf_op jit(solution)/shard_map/ppermute | solution.py:120
  14.5 1.4 %collective-permute-start.6 = (bf16[2,128,128]{2,1,0:T(8,128)(2,1)S(1)}, bf16[2,128,128]{2,1,0:T(8,128)(2,1)S(1)}, u32[]{:S(2)}, u32[]{:S(2)}) collective-permute-start(bf16[2,128,128]{2,1,0:T(8,128)(2,1)S(1)} %collective-permute-done.4.rest_5_), channel_id=1, source_target_pairs={{0,1},{1,0},{2,3},{3,2},{4,5},{5,4},{6,7},{7,6},{8,9},{9,8},{10,11... | collective-permute-start | bytes 196616 | tf_op jit(solution)/shard_map/ppermute | solution.py:120

commit v4 on v3

--- a/solution.py
+++ b/solution.py
@@ -136,11 +136,12 @@
 
 
 def block_steps(size):
-    far = list(range(size - 2, 2, -2))
-    steps = [(k, (0,)) for k in far[1:]] + [(1, (0,))] + [(k, (0,)) for k in far[:1]]
-    steps += [(2, (0, 1))] if size > 2 else []
-    far.reverse()
-    return steps + [(1, tuple(far[i:i + 2])) for i in range(0, len(far), 2)]
+    far = tuple(range(4, size, 4))
+    first = [(1, (0,))] + [(k, (0,)) for k in far]
+    last = [(2, (0, 1))] if size > 2 else []
+    if far:
+        last += [(k, far) for k in (1, 2, 3)]
+    return first, last
 
 
 def tile_steps(size):
@@ -164,7 +165,6 @@
     params = pltpu.CompilerParams(vmem_limit_bytes=LIMIT)
     DMA = pltpu.SemaphoreType.DMA
     tile = (pairs, width, width)
-    tables = spread(integrals, "col", tile_steps(groups))
     held = pl.pallas_call(
         hold_kernel,
         out_shape=VMEM(tile, jnp.bfloat16),
@@ -173,8 +173,12 @@
         scratch_shapes=[SMEM((pairs,), jnp.int32), VMEM(tile, jnp.bfloat16), DMA((2,))],
         compiler_params=params,
     )(put(domain[0, 0], HBM), put(amps[0, 0], HBM))
-    pieces = spread(held, "blk", block_steps(blocks))
-    early, late = pieces[:-1], pieces[-1:]
+    tables = spread(integrals, "col", tile_steps(groups))
+    first, last = block_steps(blocks)
+    pieces = spread(held, "blk", first + last)
+    ahead = len(pieces) - max(len(last), 1)
+    early, late = pieces[:ahead], pieces[ahead:]
+    late = late[-1:] + late[1:-1] + late[:1] if len(late) > 1 else late
     place = lax.axis_index("blk").reshape(1)
     ring = lax.axis_index("col").reshape(1)
     loffs = [off for offs, _ in late for off in offs]

time: 30.4 us -> 29.7 us (0.977)
  waiting for transfers between devices: 6.24 us -> 3.63 us
  starting transfers between devices: 9.84 us -> 12.2 us
  blocking collectives: 10.3 us -> 9.78 us
    ppermute x8 -> x9, waiting for transfers between devices: 6.24 us -> 3.63 us  [xor(): lax.ppermute(v, axis, [(i, i ^ k) for i in range(lax.axis_size(axis))])]
    ppermute x8 -> x9, starting transfers between devices: 9.84 us -> 12.2 us  [xor(): lax.ppermute(v, axis, [(i, i ^ k) for i in range(lax.axis_size(axis))])]
    all_to_all x1, blocking collectives: 10.3 us -> 9.78 us  [per_device(): rows = lax.all_to_all(squares, ('blk', 'col'), 0, 0, tiled=True)]
  transfers between devices with their start and end apart: 8 -> 9, of which waited for: 4 -> 4; matrix products, arithmetic and copies ran while one was open for 0% -> 0% of each run, Pallas kernels for 4% -> 4%
where the time goes in v4:
time: 29.7 us; the launch traced here: 29.5 us
  starting transfers between devices  12.2 us (41%)
  blocking collectives  9.78 us (33%)
  waiting for transfers between devices  3.63 us (12%)
  Pallas kernels  3.18 us (11%)
  between operations  0.67 us (2%)
    ppermute x9, starting transfers between devices, xor(): lax.ppermute(v, axis, [(i, i ^ k) for i in range(lax.axis_size(axis))])  12.2 us
    all_to_all x1, blocking collectives, per_device(): rows = lax.all_to_all(squares, ('blk', 'col'), 0, 0, tiled=True)  9.78 us
    ppermute x9, waiting for transfers between devices, xor(): lax.ppermute(v, axis, [(i, i ^ k) for i in range(lax.axis_size(axis))])  3.63 us
    pallas_call x1, Pallas kernels, per_device(): pl.pallas_call(functools.partial(early_kernel, [o for o, _ in early], lof...  1.29 us
    pallas_call x1, Pallas kernels, per_device(): pl.pallas_call(hold_kernel, out_shape=VMEM(tile, jnp.bfloat16), in_specs=...  0.92 us
    pallas_call x1, Pallas kernels, per_device(): pl.pallas_call(functools.partial(finish_kernel, entries), out_shape=[jax....  0.68 us
  transfers between devices with their start and end apart: 9, of which 4 were waited for; matrix products, arithmetic and copies ran while one was open for 0% of the time, Pallas kernels for 4%

profile of v4, /device:TPU:0, one launch (start us, length us, event | category | flops | bytes accessed | tf_op | source)
XLA Modules:
  0.0 29.5 jit_solution(352803014161765293)
XLA Ops:
  0.6 0.0 copy-start
  0.6 0.9 %shard_map.86.rest_0_.held = bf16[2,128,128]{2,1,0:T(8,128)(2,1)S(1)} custom-call(s32[2]{0:T(128)} %bitcast.21, bf16[2,128,128]{2,1,0:T(8,128)(2,1)} %bitcast.19), custom_call_target="tpu_custom_call" | custom-call | tf_op jit(solution)/shard_map/pallas_call | solution.py:168
  1.6 3.0 %collective-permute-start = (bf16[2,128,128]{2,1,0:T(8,128)(2,1)S(1)}, bf16[2,128,128]{2,1,0:T(8,128)(2,1)S(1)}, u32[]{:S(2)}, u32[]{:S(2)}) collective-permute-start(bf16[2,128,128]{2,1,0:T(8,128)(2,1)S(1)} %shard_map.86.rest_0_.held), channel_id=1, source_target_pairs={{0,4},{4,0},{8,12},{12,8},{16,20},{20,16},{24,28},{28,24},{1,5},{5... | collective-permute-start | bytes 196616 | tf_op jit(solution)/shard_map/ppermute | solution.py:120
  4.6 2.6 %collective-permute-start.1 = (bf16[2,128,128]{2,1,0:T(8,128)(2,1)S(1)}, bf16[2,128,128]{2,1,0:T(8,128)(2,1)S(1)}, u32[]{:S(2)}, u32[]{:S(2)}) collective-permute-start(bf16[2,128,128]{2,1,0:T(8,128)(2,1)S(1)} %shard_map.86.rest_0_.held), channel_id=1, source_target_pairs={{0,16},{4,20},{8,24},{12,28},{16,0},{20,4},{24,8},{28,12},{1,17},{... | collective-permute-start | bytes 196616 | tf_op jit(solution)/shard_map/ppermute | solution.py:120
  7.2 0.0 copy-done
  7.2 1.5 %collective-permute-start.2 = (bf16[2,128,128]{2,1,0:T(8,128)(2,1)S(1)}, bf16[2,128,128]{2,1,0:T(8,128)(2,1)S(1)}, u32[]{:S(2)}, u32[]{:S(2)}) collective-permute-start(bf16[2,128,128]{2,1,0:T(8,128)(2,1)S(1)} %copy-done), channel_id=1, source_target_pairs={{0,2},{1,3},{2,0},{3,1},{4,6},{5,7},{6,4},{7,5},{8,10},{9,11},{10,... | collective-permute-start | bytes 196616 | tf_op jit(solution)/shard_map/ppermute | solution.py:120
  8.7 0.0 collective-permute-start.3
  8.7 0.0 collective-permute-done.rest_1_
  8.7 1.6 %collective-permute-start.8 = (bf16[4,128,128]{2,1,0:T(8,128)(2,1)S(1)}, bf16[4,128,128]{2,1,0:T(8,128)(2,1)S(1)}, u32[]{:S(2)}, u32[]{:S(2)}) collective-permute-start(bf16[4,128,128]{2,1,0:T(8,128)(2,1)S(1)} %pad_maximum_fusion), channel_id=1, source_target_pairs={{0,8},{4,12},{8,0},{12,4},{16,24},{20,28},{24,16},{28,20},{1,9},{5... | collective-permute-start | bytes 393224 | tf_op jit(solution)/shard_map/ppermute | solution.py:120
  10.3 1.1 %collective-permute-done.2.rest_3_ = bf16[2,128,128]{2,1,0:T(8,128)(2,1)S(1)} collective-permute-done((bf16[2,128,128]{2,1,0:T(8,128)(2,1)S(1)}, bf16[2,128,128]{2,1,0:T(8,128)(2,1)S(1)}, u32[]{:S(2)}, u32[]{:S(2)}) %collective-permute-start.2) | collective-permute-done | bytes 65568 | tf_op jit(solution)/shard_map/ppermute | solution.py:120
  11.5 0.0 collective-permute-start.4
  11.5 0.0 collective-permute-done.1.rest_2_
  11.5 1.5 %collective-permute-start.5 = (bf16[2,128,128]{2,1,0:T(8,128)(2,1)S(1)}, bf16[2,128,128]{2,1,0:T(8,128)(2,1)S(1)}, u32[]{:S(2)}, u32[]{:S(2)}) collective-permute-start(bf16[2,128,128]{2,1,0:T(8,128)(2,1)S(1)} %collective-permute-done.1.rest_2_), channel_id=1, source_target_pairs={{0,12},{4,8},{8,4},{12,0},{16,28},{20,24},{24,20},{28,16},{1,13},{... | collective-permute-start | bytes 196616 | tf_op jit(solution)/shard_map/ppermute | solution.py:120
  13.0 1.5 %collective-permute-start.6 = (bf16[2,128,128]{2,1,0:T(8,128)(2,1)S(1)}, bf16[2,128,128]{2,1,0:T(8,128)(2,1)S(1)}, u32[]{:S(2)}, u32[]{:S(2)}) collective-permute-start(bf16[2,128,128]{2,1,0:T(8,128)(2,1)S(1)} %collective-permute-done.1.rest_2_), channel_id=1, source_target_pairs={{0,4},{4,0},{8,12},{12,8},{16,20},{20,16},{24,28},{28,24},{1,5},{5... | collective-permute-start | bytes 196616 | tf_op jit(solution)/shard_map/ppermute | solution.py:120
  14.5 0.0 collective-permute-done.3.rest_4_
  14.5 0.5 %collective-permute-start.7 = (bf16[2,128,128]{2,1,0:T(8,128)(2,1)S(1)}, bf16[2,128,128]{2,1,0:T(8,128)(2,1)S(1)}, u32[]{:S(2)}, u32[]{:S(2)}) collective-permute-start(bf16[2,128,128]{2,1,0:T(8,128)(2,1)S(1)} %collective-permute-done.1.rest_2_), channel_id=1, source_target_pairs={{0,8},{4,12},{8,0},{12,4},{16,24},{20,28},{24,16},{28,20},{1,9},{5... | collective-permute-start | bytes 196616 | tf_op jit(solution)/shard_map/ppermute | solution.py:120
  15.0 0.0 collective-permute-done.4.rest_5_
  15.0 1.3 %shard_map.87 = (bf16[1280,256]{1,0:T(8,128)(2,1)S(1)}, f32[2,128,128]{2,1,0:T(8,128)S(1)}, f32[2,128,128]{2,1,0:T(8,128)S(1)}, f32[2,128,128]{2,1,0:T(8,128)S(1)}) custom-call(s32[1]{0:T(128)} %bitcast.place, s32[1]{0:T(128)} %bitcast.1.ring, s32[2,2,8]{2,1,0:T(2,128)} %bitcast.20, s32[2]{0:T(128)} %bitcast.22, f32[2]{0:T(128)} %bitcast.24, ...), custom_call_target="tpu_custom_call" | custom-call | tf_op jit(solution)/shard_map/pallas_call | solution.py:188
  16.3 0.7 %collective-permute-done.5.rest_0_ = bf16[2,128,128]{2,1,0:T(8,128)(2,1)S(1)} collective-permute-done((bf16[2,128,128]{2,1,0:T(8,128)(2,1)S(1)}, bf16[2,128,128]{2,1,0:T(8,128)(2,1)S(1)}, u32[]{:S(2)}, u32[]{:S(2)}) %collective-permute-start.5) | collective-permute-done | bytes 65568 | tf_op jit(solution)/shard_map/ppermute | solution.py:120
  17.0 1.3 %collective-permute-done.6.rest_1_ = bf16[2,128,128]{2,1,0:T(8,128)(2,1)S(1)} collective-permute-done((bf16[2,128,128]{2,1,0:T(8,128)(2,1)S(1)}, bf16[2,128,128]{2,1,0:T(8,128)(2,1)S(1)}, u32[]{:S(2)}, u32[]{:S(2)}) %collective-permute-start.6) | collective-permute-done | bytes 65568 | tf_op jit(solution)/shard_map/ppermute | solution.py:120
  18.3 0.5 %collective-permute-done.7.rest_2_ = bf16[2,128,128]{2,1,0:T(8,128)(2,1)S(1)} collective-permute-done((bf16[2,128,128]{2,1,0:T(8,128)(2,1)S(1)}, bf16[2,128,128]{2,1,0:T(8,128)(2,1)S(1)}, u32[]{:S(2)}, u32[]{:S(2)}) %collective-permute-start.7) | collective-permute-done | bytes 65568 | tf_op jit(solution)/shard_map/ppermute | solution.py:120
  18.8 0.0 collective-permute-done.8.rest_3_
  18.8 0.3 shard_map.88
  19.1 9.8 %all_to_all.11 = f32[32,1,128]{2,1,0:T(1,128)S(1)} all-to-all(f32[32,1,128]{2,1,0:T(1,128)S(1)} %bitcast.17), channel_id=1, replica_groups=mesh['blk'=8,'col'=4] {'blk','col'}, dimensions={0} | all-to-all | bytes 32768 | tf_op jit(solution)/shard_map/all_to_all | solution.py:212
  28.8 0.7 %shard_map.89 = (f32[2,128,128]{2,1,0:T(8,128)}, f32[1,1]{1,0:T(1,128)}) custom-call(f32[32,128]{1,0:T(8,128)S(1)} %bitcast.16, bf16[2,128,128]{2,1,0:T(8,128)(2,1)S(1)} %shard_map.86.rest_0_.held, f32[2,128,128]{2,1,0:T(8,128)S(1)} %get-tuple-element.14.resid, f32[2,128,128]{2,1,0:T(8,128)S(1)} %get-tuple-element.15.inverse), custom_call_target="tpu_custom_call" | custom-call | tf_op jit(solution)/shard_map/pallas_call | solution.py:213
  (1 shorter events, 0.0 us)
Async XLA Ops:
  0.6 6.6 %copy-start = (bf16[2,128,128]{2,1,0:T(8,128)(2,1)S(1)}, bf16[2,128,128]{2,1,0:T(8,128)(2,1)}, u32[]{:S(2)}) copy-start(bf16[2,128,128]{2,1,0:T(8,128)(2,1)} %own_in.1) | copy-start | bytes 196612
  1.6 7.1 %collective-permute-start = (bf16[2,128,128]{2,1,0:T(8,128)(2,1)S(1)}, bf16[2,128,128]{2,1,0:T(8,128)(2,1)S(1)}, u32[]{:S(2)}, u32[]{:S(2)}) collective-permute-start(bf16[2,128,128]{2,1,0:T(8,128)(2,1)S(1)} %shard_map.86.rest_0_.held), channel_id=1, source_target_pairs={{0,4},{4,0},{8,12},{12,8},{16,20},{20,16},{24,28},{28,24},{1,5},{5... | collective-permute-start | bytes 196616 | tf_op jit(solution)/shard_map/ppermute | solution.py:120
  4.6 6.9 %collective-permute-start.1 = (bf16[2,128,128]{2,1,0:T(8,128)(2,1)S(1)}, bf16[2,128,128]{2,1,0:T(8,128)(2,1)S(1)}, u32[]{:S(2)}, u32[]{:S(2)}) collective-permute-start(bf16[2,128,128]{2,1,0:T(8,128)(2,1)S(1)} %shard_map.86.rest_0_.held), channel_id=1, source_target_pairs={{0,16},{4,20},{8,24},{12,28},{16,0},{20,4},{24,8},{28,12},{1,17},{... | collective-permute-start | bytes 196616 | tf_op jit(solution)/shard_map/ppermute | solution.py:120
  7.2 4.3 %collective-permute-start.2 = (bf16[2,128,128]{2,1,0:T(8,128)(2,1)S(1)}, bf16[2,128,128]{2,1,0:T(8,128)(2,1)S(1)}, u32[]{:S(2)}, u32[]{:S(2)}) collective-permute-start(bf16[2,128,128]{2,1,0:T(8,128)(2,1)S(1)} %copy-done), channel_id=1, source_target_pairs={{0,2},{1,3},{2,0},{3,1},{4,6},{5,7},{6,4},{7,5},{8,10},{9,11},{10,... | collective-permute-start | bytes 196616 | tf_op jit(solution)/shard_map/ppermute | solution.py:120
  8.7 5.8 %collective-permute-start.3 = (bf16[2,128,128]{2,1,0:T(8,128)(2,1)S(1)}, bf16[2,128,128]{2,1,0:T(8,128)(2,1)S(1)}, u32[]{:S(2)}, u32[]{:S(2)}) collective-permute-start(bf16[2,128,128]{2,1,0:T(8,128)(2,1)S(1)} %copy-done), channel_id=1, source_target_pairs={{0,1},{1,0},{2,3},{3,2},{4,5},{5,4},{6,7},{7,6},{8,9},{9,8},{10,11... | collective-permute-start | bytes 196616 | tf_op jit(solution)/shard_map/ppermute | solution.py:120
  8.7 10.1 %collective-permute-start.8 = (bf16[4,128,128]{2,1,0:T(8,128)(2,1)S(1)}, bf16[4,128,128]{2,1,0:T(8,128)(2,1)S(1)}, u32[]{:S(2)}, u32[]{:S(2)}) collective-permute-start(bf16[4,128,128]{2,1,0:T(8,128)(2,1)S(1)} %pad_maximum_fusion), channel_id=1, source_target_pairs={{0,8},{4,12},{8,0},{12,4},{16,24},{20,28},{24,16},{28,20},{1,9},{5... | collective-permute-start | bytes 393224 | tf_op jit(solution)/shard_map/ppermute | solution.py:120
  11.5 3.5 %collective-permute-start.4 = (bf16[2,128,128]{2,1,0:T(8,128)(2,1)S(1)}, bf16[2,128,128]{2,1,0:T(8,128)(2,1)S(1)}, u32[]{:S(2)}, u32[]{:S(2)}) collective-permute-start(bf16[2,128,128]{2,1,0:T(8,128)(2,1)S(1)} %collective-permute-done.2.rest_3_), channel_id=1, source_target_pairs={{0,1},{1,0},{2,3},{3,2},{4,5},{5,4},{6,7},{7,6},{8,9},{9,8},{10,11... | collective-permute-start | bytes 196616 | tf_op jit(solution)/shard_map/ppermute | solution.py:120
  11.5 5.5 %collective-permute-start.5 = (bf16[2,128,128]{2,1,0:T(8,128)(2,1)S(1)}, bf16[2,128,128]{2,1,0:T(8,128)(2,1)S(1)}, u32[]{:S(2)}, u32[]{:S(2)}) collective-permute-start(bf16[2,128,128]{2,1,0:T(8,128)(2,1)S(1)} %collective-permute-done.1.rest_2_), channel_id=1, source_target_pairs={{0,12},{4,8},{8,4},{12,0},{16,28},{20,24},{24,20},{28,16},{1,13},{... | collective-permute-start | bytes 196616 | tf_op jit(solution)/shard_map/ppermute | solution.py:120
  13.0 5.3 %collective-permute-start.6 = (bf16[2,128,128]{2,1,0:T(8,128)(2,1)S(1)}, bf16[2,128,128]{2,1,0:T(8,128)(2,1)S(1)}, u32[]{:S(2)}, u32[]{:S(2)}) collective-permute-start(bf16[2,128,128]{2,1,0:T(8,128)(2,1)S(1)} %collective-permute-done.1.rest_2_), channel_id=1, source_target_pairs={{0,4},{4,0},{8,12},{12,8},{16,20},{20,16},{24,28},{28,24},{1,5},{5... | collective-permute-start | bytes 196616 | tf_op jit(solution)/shard_map/ppermute | solution.py:120
  14.5 4.3 %collective-permute-start.7 = (bf16[2,128,128]{2,1,0:T(8,128)(2,1)S(1)}, bf16[2,128,128]{2,1,0:T(8,128)(2,1)S(1)}, u32[]{:S(2)}, u32[]{:S(2)}) collective-permute-start(bf16[2,128,128]{2,1,0:T(8,128)(2,1)S(1)} %collective-permute-done.1.rest_2_), channel_id=1, source_target_pairs={{0,8},{4,12},{8,0},{12,4},{16,24},{20,28},{24,16},{28,20},{1,9},{5... | collective-permute-start | bytes 196616 | tf_op jit(solution)/shard_map/ppermute | solution.py:120

commit v5 on v4

--- a/solution.py
+++ b/solution.py
@@ -21,16 +21,16 @@
 
 
 def hold_kernel(domain_in, amps_in, held, domain, amps, sem):
-    copies = [
-        pltpu.make_async_copy(domain_in, domain, sem.at[0]),
-        pltpu.make_async_copy(amps_in, amps, sem.at[1]),
-    ]
+    pairs = amps.shape[0]
+    copies = [pltpu.make_async_copy(amps_in.at[p], amps.at[p], sem.at[p]) for p in range(pairs)]
+    limit = pltpu.make_async_copy(domain_in, domain, sem.at[pairs])
+    limit.start()
     for copy in copies:
         copy.start()
-    for copy in copies:
-        copy.wait()
-    for p in range(amps.shape[0]):
+    limit.wait()
+    for p in range(pairs):
         inside = edges(amps.shape[-1], domain[p])
+        copies[p].wait()
         held[p] = jnp.where(inside, amps[p].astype(jnp.float32), 0.0).astype(held.dtype)
 
 
@@ -146,7 +146,7 @@
 
 def tile_steps(size):
     far = range(2, size, 2)
-    return [(k, (0,)) for k in far] + [(1, (0,))] + [(1, (k,)) for k in far]
+    return [(1, (0,))] + [(k + 1, (0,)) for k in far] + [(k, (0,)) for k in far]
 
 
 def put(x, space):
@@ -170,7 +170,7 @@
         out_shape=VMEM(tile, jnp.bfloat16),
         in_specs=[spec(HBM)] * 2,
         out_specs=spec(VMEM),
-        scratch_shapes=[SMEM((pairs,), jnp.int32), VMEM(tile, jnp.bfloat16), DMA((2,))],
+        scratch_shapes=[SMEM((pairs,), jnp.int32), VMEM(tile, jnp.bfloat16), DMA((pairs + 1,))],
         compiler_params=params,
     )(put(domain[0, 0], HBM), put(amps[0, 0], HBM))
     tables = spread(integrals, "col", tile_steps(groups))

time: 29.7 us -> 29.7 us (level)
  waiting for transfers between devices: 3.63 us -> 1.4 us
  blocking collectives: 9.78 us -> 11.4 us
  starting transfers between devices: 12.2 us -> 12.9 us
    ppermute x9, waiting for transfers between devices: 3.63 us -> 1.4 us  [xor(): lax.ppermute(v, axis, [(i, i ^ k) for i in range(lax.axis_size(axis))])]
    all_to_all x1, blocking collectives: 9.78 us -> 11.4 us  [per_device(): rows = lax.all_to_all(squares, ('blk', 'col'), 0, 0, tiled=True)]
    ppermute x9, starting transfers between devices: 12.2 us -> 12.9 us  [xor(): lax.ppermute(v, axis, [(i, i ^ k) for i in range(lax.axis_size(axis))])]
where the time goes in v5:
time: 29.7 us; the launch traced here: 29.5 us
  starting transfers between devices  12.9 us (43%)
  blocking collectives  11.4 us (38%)
  Pallas kernels  3.12 us (11%)
  waiting for transfers between devices  1.4 us (5%)
  between operations  0.67 us (2%)
    ppermute x9, starting transfers between devices, xor(): lax.ppermute(v, axis, [(i, i ^ k) for i in range(lax.axis_size(axis))])  12.9 us
    all_to_all x1, blocking collectives, per_device(): rows = lax.all_to_all(squares, ('blk', 'col'), 0, 0, tiled=True)  11.4 us
    ppermute x9, waiting for transfers between devices, xor(): lax.ppermute(v, axis, [(i, i ^ k) for i in range(lax.axis_size(axis))])  1.4 us
    pallas_call x1, Pallas kernels, per_device(): pl.pallas_call(functools.partial(early_kernel, [o for o, _ in early], lof...  1.29 us
    pallas_call x1, Pallas kernels, per_device(): pl.pallas_call(hold_kernel, out_shape=VMEM(tile, jnp.bfloat16), in_specs=...  0.86 us
    pallas_call x1, Pallas kernels, per_device(): pl.pallas_call(functools.partial(finish_kernel, entries), out_shape=[jax....  0.68 us
  transfers between devices with their start and end apart: 9, of which 4 were waited for; matrix products, arithmetic and copies ran while one was open for 0% of the time, Pallas kernels for 4%

profile of v5, /device:TPU:0, one launch (start us, length us, event | category | flops | bytes accessed | tf_op | source)
XLA Modules:
  0.0 29.5 jit_solution(5805778868723021531)
XLA Ops:
  0.6 0.0 copy-start
  0.6 0.9 %shard_map.86.rest_0_.held = bf16[2,128,128]{2,1,0:T(8,128)(2,1)S(1)} custom-call(s32[2]{0:T(128)} %bitcast.21, bf16[2,128,128]{2,1,0:T(8,128)(2,1)} %bitcast.19), custom_call_target="tpu_custom_call" | custom-call | tf_op jit(solution)/shard_map/pallas_call | solution.py:168
  1.5 3.0 %collective-permute-start = (bf16[2,128,128]{2,1,0:T(8,128)(2,1)S(1)}, bf16[2,128,128]{2,1,0:T(8,128)(2,1)S(1)}, u32[]{:S(2)}, u32[]{:S(2)}) collective-permute-start(bf16[2,128,128]{2,1,0:T(8,128)(2,1)S(1)} %shard_map.86.rest_0_.held), channel_id=1, source_target_pairs={{0,4},{4,0},{8,12},{12,8},{16,20},{20,16},{24,28},{28,24},{1,5},{5... | collective-permute-start | bytes 196616 | tf_op jit(solution)/shard_map/ppermute | solution.py:120
  4.5 2.6 %collective-permute-start.1 = (bf16[2,128,128]{2,1,0:T(8,128)(2,1)S(1)}, bf16[2,128,128]{2,1,0:T(8,128)(2,1)S(1)}, u32[]{:S(2)}, u32[]{:S(2)}) collective-permute-start(bf16[2,128,128]{2,1,0:T(8,128)(2,1)S(1)} %shard_map.86.rest_0_.held), channel_id=1, source_target_pairs={{0,16},{4,20},{8,24},{12,28},{16,0},{20,4},{24,8},{28,12},{1,17},{... | collective-permute-start | bytes 196616 | tf_op jit(solution)/shard_map/ppermute | solution.py:120
  7.1 0.0 copy-done
  7.1 0.0 collective-permute-start.2
  7.1 1.6 %collective-permute-start.3 = (bf16[2,128,128]{2,1,0:T(8,128)(2,1)S(1)}, bf16[2,128,128]{2,1,0:T(8,128)(2,1)S(1)}, u32[]{:S(2)}, u32[]{:S(2)}) collective-permute-start(bf16[2,128,128]{2,1,0:T(8,128)(2,1)S(1)} %copy-done), channel_id=1, source_target_pairs={{0,3},{1,2},{2,1},{3,0},{4,7},{5,6},{6,5},{7,4},{8,11},{9,10},{10,... | collective-permute-start | bytes 196616 | tf_op jit(solution)/shard_map/ppermute | solution.py:120
  8.7 0.0 collective-permute-done.rest_1_
  8.8 1.6 %collective-permute-start.8 = (bf16[4,128,128]{2,1,0:T(8,128)(2,1)S(1)}, bf16[4,128,128]{2,1,0:T(8,128)(2,1)S(1)}, u32[]{:S(2)}, u32[]{:S(2)}) collective-permute-start(bf16[4,128,128]{2,1,0:T(8,128)(2,1)S(1)} %pad_maximum_fusion), channel_id=1, source_target_pairs={{0,8},{4,12},{8,0},{12,4},{16,24},{20,28},{24,16},{28,20},{1,9},{5... | collective-permute-start | bytes 393224 | tf_op jit(solution)/shard_map/ppermute | solution.py:120
  10.4 0.5 %collective-permute-start.4 = (bf16[2,128,128]{2,1,0:T(8,128)(2,1)S(1)}, bf16[2,128,128]{2,1,0:T(8,128)(2,1)S(1)}, u32[]{:S(2)}, u32[]{:S(2)}) collective-permute-start(bf16[2,128,128]{2,1,0:T(8,128)(2,1)S(1)} %copy-done), channel_id=1, source_target_pairs={{0,2},{1,3},{2,0},{3,1},{4,6},{5,7},{6,4},{7,5},{8,10},{9,11},{10,... | collective-permute-start | bytes 196616 | tf_op jit(solution)/shard_map/ppermute | solution.py:120
  10.9 0.0 collective-permute-done.1.rest_2_
  10.9 0.9 %collective-permute-start.5 = (bf16[2,128,128]{2,1,0:T(8,128)(2,1)S(1)}, bf16[2,128,128]{2,1,0:T(8,128)(2,1)S(1)}, u32[]{:S(2)}, u32[]{:S(2)}) collective-permute-start(bf16[2,128,128]{2,1,0:T(8,128)(2,1)S(1)} %collective-permute-done.1.rest_2_), channel_id=1, source_target_pairs={{0,12},{4,8},{8,4},{12,0},{16,28},{20,24},{24,20},{28,16},{1,13},{... | collective-permute-start | bytes 196616 | tf_op jit(solution)/shard_map/ppermute | solution.py:120
  11.8 0.0 collective-permute-done.2.rest_3_
  11.9 1.0 %collective-permute-start.6 = (bf16[2,128,128]{2,1,0:T(8,128)(2,1)S(1)}, bf16[2,128,128]{2,1,0:T(8,128)(2,1)S(1)}, u32[]{:S(2)}, u32[]{:S(2)}) collective-permute-start(bf16[2,128,128]{2,1,0:T(8,128)(2,1)S(1)} %collective-permute-done.1.rest_2_), channel_id=1, source_target_pairs={{0,4},{4,0},{8,12},{12,8},{16,20},{20,16},{24,28},{28,24},{1,5},{5... | collective-permute-start | bytes 196616 | tf_op jit(solution)/shard_map/ppermute | solution.py:120
  12.9 0.0 collective-permute-done.3.rest_4_
  12.9 1.6 %collective-permute-start.7 = (bf16[2,128,128]{2,1,0:T(8,128)(2,1)S(1)}, bf16[2,128,128]{2,1,0:T(8,128)(2,1)S(1)}, u32[]{:S(2)}, u32[]{:S(2)}) collective-permute-start(bf16[2,128,128]{2,1,0:T(8,128)(2,1)S(1)} %collective-permute-done.1.rest_2_), channel_id=1, source_target_pairs={{0,8},{4,12},{8,0},{12,4},{16,24},{20,28},{24,16},{28,20},{1,9},{5... | collective-permute-start | bytes 196616 | tf_op jit(solution)/shard_map/ppermute | solution.py:120
  14.4 0.2 collective-permute-done.4.rest_5_
  14.7 1.3 %shard_map.87 = (bf16[1280,256]{1,0:T(8,128)(2,1)S(1)}, f32[2,128,128]{2,1,0:T(8,128)S(1)}, f32[2,128,128]{2,1,0:T(8,128)S(1)}, f32[2,128,128]{2,1,0:T(8,128)S(1)}) custom-call(s32[1]{0:T(128)} %bitcast.place, s32[1]{0:T(128)} %bitcast.1.ring, s32[2,2,8]{2,1,0:T(2,128)} %bitcast.20, s32[2]{0:T(128)} %bitcast.22, f32[2]{0:T(128)} %bitcast.24, ...), custom_call_target="tpu_custom_call" | custom-call | tf_op jit(solution)/shard_map/pallas_call | solution.py:188
  16.0 0.4 %collective-permute-done.5.rest_0_ = bf16[2,128,128]{2,1,0:T(8,128)(2,1)S(1)} collective-permute-done((bf16[2,128,128]{2,1,0:T(8,128)(2,1)S(1)}, bf16[2,128,128]{2,1,0:T(8,128)(2,1)S(1)}, u32[]{:S(2)}, u32[]{:S(2)}) %collective-permute-start.5) | collective-permute-done | bytes 65568 | tf_op jit(solution)/shard_map/ppermute | solution.py:120
  16.4 0.4 %collective-permute-done.6.rest_1_ = bf16[2,128,128]{2,1,0:T(8,128)(2,1)S(1)} collective-permute-done((bf16[2,128,128]{2,1,0:T(8,128)(2,1)S(1)}, bf16[2,128,128]{2,1,0:T(8,128)(2,1)S(1)}, u32[]{:S(2)}, u32[]{:S(2)}) %collective-permute-start.6) | collective-permute-done | bytes 65568 | tf_op jit(solution)/shard_map/ppermute | solution.py:120
  16.8 0.3 %collective-permute-done.7.rest_2_ = bf16[2,128,128]{2,1,0:T(8,128)(2,1)S(1)} collective-permute-done((bf16[2,128,128]{2,1,0:T(8,128)(2,1)S(1)}, bf16[2,128,128]{2,1,0:T(8,128)(2,1)S(1)}, u32[]{:S(2)}, u32[]{:S(2)}) %collective-permute-start.7) | collective-permute-done | bytes 65568 | tf_op jit(solution)/shard_map/ppermute | solution.py:120
  17.1 0.0 collective-permute-done.8.rest_3_
  17.1 0.3 shard_map.88
  17.4 11.4 %all_to_all.11 = f32[32,1,128]{2,1,0:T(1,128)S(1)} all-to-all(f32[32,1,128]{2,1,0:T(1,128)S(1)} %bitcast.17), channel_id=1, replica_groups=mesh['blk'=8,'col'=4] {'blk','col'}, dimensions={0} | all-to-all | bytes 32768 | tf_op jit(solution)/shard_map/all_to_all | solution.py:212
  28.8 0.7 %shard_map.89 = (f32[2,128,128]{2,1,0:T(8,128)}, f32[1,1]{1,0:T(1,128)}) custom-call(f32[32,128]{1,0:T(8,128)S(1)} %bitcast.16, bf16[2,128,128]{2,1,0:T(8,128)(2,1)S(1)} %shard_map.86.rest_0_.held, f32[2,128,128]{2,1,0:T(8,128)S(1)} %get-tuple-element.14.resid, f32[2,128,128]{2,1,0:T(8,128)S(1)} %get-tuple-element.15.inverse), custom_call_target="tpu_custom_call" | custom-call | tf_op jit(solution)/shard_map/pallas_call | solution.py:213
  (1 shorter events, 0.0 us)
Async XLA Ops:
  0.6 6.5 %copy-start = (bf16[2,128,128]{2,1,0:T(8,128)(2,1)S(1)}, bf16[2,128,128]{2,1,0:T(8,128)(2,1)}, u32[]{:S(2)}) copy-start(bf16[2,128,128]{2,1,0:T(8,128)(2,1)} %own_in.1) | copy-start | bytes 196612
  1.5 7.2 %collective-permute-start = (bf16[2,128,128]{2,1,0:T(8,128)(2,1)S(1)}, bf16[2,128,128]{2,1,0:T(8,128)(2,1)S(1)}, u32[]{:S(2)}, u32[]{:S(2)}) collective-permute-start(bf16[2,128,128]{2,1,0:T(8,128)(2,1)S(1)} %shard_map.86.rest_0_.held), channel_id=1, source_target_pairs={{0,4},{4,0},{8,12},{12,8},{16,20},{20,16},{24,28},{28,24},{1,5},{5... | collective-permute-start | bytes 196616 | tf_op jit(solution)/shard_map/ppermute | solution.py:120
  4.5 6.4 %collective-permute-start.1 = (bf16[2,128,128]{2,1,0:T(8,128)(2,1)S(1)}, bf16[2,128,128]{2,1,0:T(8,128)(2,1)S(1)}, u32[]{:S(2)}, u32[]{:S(2)}) collective-permute-start(bf16[2,128,128]{2,1,0:T(8,128)(2,1)S(1)} %shard_map.86.rest_0_.held), channel_id=1, source_target_pairs={{0,16},{4,20},{8,24},{12,28},{16,0},{20,4},{24,8},{28,12},{1,17},{... | collective-permute-start | bytes 196616 | tf_op jit(solution)/shard_map/ppermute | solution.py:120
  7.1 4.7 %collective-permute-start.2 = (bf16[2,128,128]{2,1,0:T(8,128)(2,1)S(1)}, bf16[2,128,128]{2,1,0:T(8,128)(2,1)S(1)}, u32[]{:S(2)}, u32[]{:S(2)}) collective-permute-start(bf16[2,128,128]{2,1,0:T(8,128)(2,1)S(1)} %copy-done), channel_id=1, source_target_pairs={{0,1},{1,0},{2,3},{3,2},{4,5},{5,4},{6,7},{7,6},{8,9},{9,8},{10,11... | collective-permute-start | bytes 196616 | tf_op jit(solution)/shard_map/ppermute | solution.py:120
  7.1 5.7 %collective-permute-start.3 = (bf16[2,128,128]{2,1,0:T(8,128)(2,1)S(1)}, bf16[2,128,128]{2,1,0:T(8,128)(2,1)S(1)}, u32[]{:S(2)}, u32[]{:S(2)}) collective-permute-start(bf16[2,128,128]{2,1,0:T(8,128)(2,1)S(1)} %copy-done), channel_id=1, source_target_pairs={{0,3},{1,2},{2,1},{3,0},{4,7},{5,6},{6,5},{7,4},{8,11},{9,10},{10,... | collective-permute-start | bytes 196616 | tf_op jit(solution)/shard_map/ppermute | solution.py:120
  8.8 8.4 %collective-permute-start.8 = (bf16[4,128,128]{2,1,0:T(8,128)(2,1)S(1)}, bf16[4,128,128]{2,1,0:T(8,128)(2,1)S(1)}, u32[]{:S(2)}, u32[]{:S(2)}) collective-permute-start(bf16[4,128,128]{2,1,0:T(8,128)(2,1)S(1)} %pad_maximum_fusion), channel_id=1, source_target_pairs={{0,8},{4,12},{8,0},{12,4},{16,24},{20,28},{24,16},{28,20},{1,9},{5... | collective-permute-start | bytes 393224 | tf_op jit(solution)/shard_map/ppermute | solution.py:120
  10.4 4.3 %collective-permute-start.4 = (bf16[2,128,128]{2,1,0:T(8,128)(2,1)S(1)}, bf16[2,128,128]{2,1,0:T(8,128)(2,1)S(1)}, u32[]{:S(2)}, u32[]{:S(2)}) collective-permute-start(bf16[2,128,128]{2,1,0:T(8,128)(2,1)S(1)} %copy-done), channel_id=1, source_target_pairs={{0,2},{1,3},{2,0},{3,1},{4,6},{5,7},{6,4},{7,5},{8,10},{9,11},{10,... | collective-permute-start | bytes 196616 | tf_op jit(solution)/shard_map/ppermute | solution.py:120
  10.9 5.4 %collective-permute-start.5 = (bf16[2,128,128]{2,1,0:T(8,128)(2,1)S(1)}, bf16[2,128,128]{2,1,0:T(8,128)(2,1)S(1)}, u32[]{:S(2)}, u32[]{:S(2)}) collective-permute-start(bf16[2,128,128]{2,1,0:T(8,128)(2,1)S(1)} %collective-permute-done.1.rest_2_), channel_id=1, source_target_pairs={{0,12},{4,8},{8,4},{12,0},{16,28},{20,24},{24,20},{28,16},{1,13},{... | collective-permute-start | bytes 196616 | tf_op jit(solution)/shard_map/ppermute | solution.py:120
  11.9 5.0 %collective-permute-start.6 = (bf16[2,128,128]{2,1,0:T(8,128)(2,1)S(1)}, bf16[2,128,128]{2,1,0:T(8,128)(2,1)S(1)}, u32[]{:S(2)}, u32[]{:S(2)}) collective-permute-start(bf16[2,128,128]{2,1,0:T(8,128)(2,1)S(1)} %collective-permute-done.1.rest_2_), channel_id=1, source_target_pairs={{0,4},{4,0},{8,12},{12,8},{16,20},{20,16},{24,28},{28,24},{1,5},{5... | collective-permute-start | bytes 196616 | tf_op jit(solution)/shard_map/ppermute | solution.py:120
  12.9 4.3 %collective-permute-start.7 = (bf16[2,128,128]{2,1,0:T(8,128)(2,1)S(1)}, bf16[2,128,128]{2,1,0:T(8,128)(2,1)S(1)}, u32[]{:S(2)}, u32[]{:S(2)}) collective-permute-start(bf16[2,128,128]{2,1,0:T(8,128)(2,1)S(1)} %collective-permute-done.1.rest_2_), channel_id=1, source_target_pairs={{0,8},{4,12},{8,0},{12,4},{16,24},{20,28},{24,16},{28,20},{1,9},{5... | collective-permute-start | bytes 196616 | tf_op jit(solution)/shard_map/ppermute | solution.py:120

commit v6 on v5

--- a/solution.py
+++ b/solution.py
@@ -109,11 +109,17 @@
     squares[...] = jnp.broadcast_to(total, squares.shape)
 
 
-def finish_kernel(entries, rows, held, resid, inverse, new, rms):
-    new[...] = held[...].astype(jnp.float32) + resid[...] * inverse[...]
+def finish_kernel(entries, rows, held, resid, inverse, new_out, rms, new, sem):
+    copies = []
+    for p in range(new.shape[0]):
+        new[p] = held[p].astype(jnp.float32) + resid[p] * inverse[p]
+        copies.append(pltpu.make_async_copy(new.at[p], new_out.at[p], sem.at[p]))
+        copies[p].start()
     total = jnp.sum(rows[...], axis=0, keepdims=True)
     total = jnp.sum(total, axis=1, keepdims=True)
     rms[...] = jnp.sqrt(total / entries)
+    for copy in copies:
+        copy.wait()
 
 
 def xor(v, axis, k):
@@ -214,7 +220,8 @@
         functools.partial(finish_kernel, entries),
         out_shape=[jax.ShapeDtypeStruct(tile, jnp.float32), jax.ShapeDtypeStruct((1, 1), jnp.float32)],
         in_specs=[spec(VMEM)] * 4,
-        out_specs=[spec(VMEM)] * 2,
+        out_specs=[spec(HBM), spec(VMEM)],
+        scratch_shapes=[VMEM(tile, jnp.float32), DMA((pairs,))],
         compiler_params=params,
     )(*[put(v, VMEM) for v in (rows, held, resid, inverse)])
     return (new[None, None], rms.reshape(()))

time: 29.7 us -> 30.2 us (1.017)
  Pallas kernels: 3.12 us -> 3.63 us
    pallas_call x1, Pallas kernels: 0.68 us -> 1.19 us  [per_device(): pl.pallas_call(functools.partial(finish_kernel, entries), out_shape=[jax....]
where the time goes in v6:
time: 30.2 us; the launch traced here: 30 us
  starting transfers between devices  12.9 us (43%)
  blocking collectives  11.4 us (38%)
  Pallas kernels  3.63 us (12%)
  waiting for transfers between devices  1.4 us (5%)
  between operations  0.67 us (2%)
    ppermute x9, starting transfers between devices, xor(): lax.ppermute(v, axis, [(i, i ^ k) for i in range(lax.axis_size(axis))])  12.9 us
    all_to_all x1, blocking collectives, per_device(): rows = lax.all_to_all(squares, ('blk', 'col'), 0, 0, tiled=True)  11.4 us
    ppermute x9, waiting for transfers between devices, xor(): lax.ppermute(v, axis, [(i, i ^ k) for i in range(lax.axis_size(axis))])  1.4 us
    pallas_call x1, Pallas kernels, per_device(): pl.pallas_call(functools.partial(early_kernel, [o for o, _ in early], lof...  1.29 us
    pallas_call x1, Pallas kernels, per_device(): pl.pallas_call(functools.partial(finish_kernel, entries), out_shape=[jax....  1.19 us
    pallas_call x1, Pallas kernels, per_device(): pl.pallas_call(hold_kernel, out_shape=VMEM(tile, jnp.bfloat16), in_specs=...  0.86 us
  transfers between devices with their start and end apart: 9, of which 4 were waited for; matrix products, arithmetic and copies ran while one was open for 0% of the time, Pallas kernels for 4%

profile of v6, /device:TPU:0, one launch (start us, length us, event | category | flops | bytes accessed | tf_op | source)
XLA Modules:
  0.0 30.0 jit_solution(8688433491365563100)
XLA Ops:
  0.6 0.0 copy-start
  0.6 0.9 %shard_map.86.rest_0_.held = bf16[2,128,128]{2,1,0:T(8,128)(2,1)S(1)} custom-call(s32[2]{0:T(128)} %bitcast.21, bf16[2,128,128]{2,1,0:T(8,128)(2,1)} %bitcast.19), custom_call_target="tpu_custom_call" | custom-call | tf_op jit(solution)/shard_map/pallas_call | solution.py:174
  1.5 3.0 %collective-permute-start = (bf16[2,128,128]{2,1,0:T(8,128)(2,1)S(1)}, bf16[2,128,128]{2,1,0:T(8,128)(2,1)S(1)}, u32[]{:S(2)}, u32[]{:S(2)}) collective-permute-start(bf16[2,128,128]{2,1,0:T(8,128)(2,1)S(1)} %shard_map.86.rest_0_.held), channel_id=1, source_target_pairs={{0,4},{4,0},{8,12},{12,8},{16,20},{20,16},{24,28},{28,24},{1,5},{5... | collective-permute-start | bytes 196616 | tf_op jit(solution)/shard_map/ppermute | solution.py:126
  4.5 2.6 %collective-permute-start.1 = (bf16[2,128,128]{2,1,0:T(8,128)(2,1)S(1)}, bf16[2,128,128]{2,1,0:T(8,128)(2,1)S(1)}, u32[]{:S(2)}, u32[]{:S(2)}) collective-permute-start(bf16[2,128,128]{2,1,0:T(8,128)(2,1)S(1)} %shard_map.86.rest_0_.held), channel_id=1, source_target_pairs={{0,16},{4,20},{8,24},{12,28},{16,0},{20,4},{24,8},{28,12},{1,17},{... | collective-permute-start | bytes 196616 | tf_op jit(solution)/shard_map/ppermute | solution.py:126
  7.1 0.0 copy-done
  7.1 0.0 collective-permute-start.2
  7.1 1.6 %collective-permute-start.3 = (bf16[2,128,128]{2,1,0:T(8,128)(2,1)S(1)}, bf16[2,128,128]{2,1,0:T(8,128)(2,1)S(1)}, u32[]{:S(2)}, u32[]{:S(2)}) collective-permute-start(bf16[2,128,128]{2,1,0:T(8,128)(2,1)S(1)} %copy-done), channel_id=1, source_target_pairs={{0,3},{1,2},{2,1},{3,0},{4,7},{5,6},{6,5},{7,4},{8,11},{9,10},{10,... | collective-permute-start | bytes 196616 | tf_op jit(solution)/shard_map/ppermute | solution.py:126
  8.7 0.0 collective-permute-done.rest_1_
  8.8 1.6 %collective-permute-start.8 = (bf16[4,128,128]{2,1,0:T(8,128)(2,1)S(1)}, bf16[4,128,128]{2,1,0:T(8,128)(2,1)S(1)}, u32[]{:S(2)}, u32[]{:S(2)}) collective-permute-start(bf16[4,128,128]{2,1,0:T(8,128)(2,1)S(1)} %pad_maximum_fusion), channel_id=1, source_target_pairs={{0,8},{4,12},{8,0},{12,4},{16,24},{20,28},{24,16},{28,20},{1,9},{5... | collective-permute-start | bytes 393224 | tf_op jit(solution)/shard_map/ppermute | solution.py:126
  10.4 0.5 %collective-permute-start.4 = (bf16[2,128,128]{2,1,0:T(8,128)(2,1)S(1)}, bf16[2,128,128]{2,1,0:T(8,128)(2,1)S(1)}, u32[]{:S(2)}, u32[]{:S(2)}) collective-permute-start(bf16[2,128,128]{2,1,0:T(8,128)(2,1)S(1)} %copy-done), channel_id=1, source_target_pairs={{0,2},{1,3},{2,0},{3,1},{4,6},{5,7},{6,4},{7,5},{8,10},{9,11},{10,... | collective-permute-start | bytes 196616 | tf_op jit(solution)/shard_map/ppermute | solution.py:126
  10.9 0.0 collective-permute-done.1.rest_2_
  10.9 0.9 %collective-permute-start.5 = (bf16[2,128,128]{2,1,0:T(8,128)(2,1)S(1)}, bf16[2,128,128]{2,1,0:T(8,128)(2,1)S(1)}, u32[]{:S(2)}, u32[]{:S(2)}) collective-permute-start(bf16[2,128,128]{2,1,0:T(8,128)(2,1)S(1)} %collective-permute-done.1.rest_2_), channel_id=1, source_target_pairs={{0,12},{4,8},{8,4},{12,0},{16,28},{20,24},{24,20},{28,16},{1,13},{... | collective-permute-start | bytes 196616 | tf_op jit(solution)/shard_map/ppermute | solution.py:126
  11.8 0.0 collective-permute-done.2.rest_3_
  11.9 1.0 %collective-permute-start.6 = (bf16[2,128,128]{2,1,0:T(8,128)(2,1)S(1)}, bf16[2,128,128]{2,1,0:T(8,128)(2,1)S(1)}, u32[]{:S(2)}, u32[]{:S(2)}) collective-permute-start(bf16[2,128,128]{2,1,0:T(8,128)(2,1)S(1)} %collective-permute-done.1.rest_2_), channel_id=1, source_target_pairs={{0,4},{4,0},{8,12},{12,8},{16,20},{20,16},{24,28},{28,24},{1,5},{5... | collective-permute-start | bytes 196616 | tf_op jit(solution)/shard_map/ppermute | solution.py:126
  12.9 0.0 collective-permute-done.3.rest_4_
  12.9 1.6 %collective-permute-start.7 = (bf16[2,128,128]{2,1,0:T(8,128)(2,1)S(1)}, bf16[2,128,128]{2,1,0:T(8,128)(2,1)S(1)}, u32[]{:S(2)}, u32[]{:S(2)}) collective-permute-start(bf16[2,128,128]{2,1,0:T(8,128)(2,1)S(1)} %collective-permute-done.1.rest_2_), channel_id=1, source_target_pairs={{0,8},{4,12},{8,0},{12,4},{16,24},{20,28},{24,16},{28,20},{1,9},{5... | collective-permute-start | bytes 196616 | tf_op jit(solution)/shard_map/ppermute | solution.py:126
  14.4 0.2 collective-permute-done.4.rest_5_
  14.7 1.3 %shard_map.87 = (bf16[1280,256]{1,0:T(8,128)(2,1)S(1)}, f32[2,128,128]{2,1,0:T(8,128)S(1)}, f32[2,128,128]{2,1,0:T(8,128)S(1)}, f32[2,128,128]{2,1,0:T(8,128)S(1)}) custom-call(s32[1]{0:T(128)} %bitcast.place, s32[1]{0:T(128)} %bitcast.1.ring, s32[2,2,8]{2,1,0:T(2,128)} %bitcast.20, s32[2]{0:T(128)} %bitcast.22, f32[2]{0:T(128)} %bitcast.24, ...), custom_call_target="tpu_custom_call" | custom-call | tf_op jit(solution)/shard_map/pallas_call | solution.py:194
  16.0 0.4 %collective-permute-done.5.rest_0_ = bf16[2,128,128]{2,1,0:T(8,128)(2,1)S(1)} collective-permute-done((bf16[2,128,128]{2,1,0:T(8,128)(2,1)S(1)}, bf16[2,128,128]{2,1,0:T(8,128)(2,1)S(1)}, u32[]{:S(2)}, u32[]{:S(2)}) %collective-permute-start.5) | collective-permute-done | bytes 65568 | tf_op jit(solution)/shard_map/ppermute | solution.py:126
  16.4 0.4 %collective-permute-done.6.rest_1_ = bf16[2,128,128]{2,1,0:T(8,128)(2,1)S(1)} collective-permute-done((bf16[2,128,128]{2,1,0:T(8,128)(2,1)S(1)}, bf16[2,128,128]{2,1,0:T(8,128)(2,1)S(1)}, u32[]{:S(2)}, u32[]{:S(2)}) %collective-permute-start.6) | collective-permute-done | bytes 65568 | tf_op jit(solution)/shard_map/ppermute | solution.py:126
  16.8 0.3 %collective-permute-done.7.rest_2_ = bf16[2,128,128]{2,1,0:T(8,128)(2,1)S(1)} collective-permute-done((bf16[2,128,128]{2,1,0:T(8,128)(2,1)S(1)}, bf16[2,128,128]{2,1,0:T(8,128)(2,1)S(1)}, u32[]{:S(2)}, u32[]{:S(2)}) %collective-permute-start.7) | collective-permute-done | bytes 65568 | tf_op jit(solution)/shard_map/ppermute | solution.py:126
  17.1 0.0 collective-permute-done.8.rest_3_
  17.1 0.3 shard_map.88
  17.4 11.4 %all_to_all.11 = f32[32,1,128]{2,1,0:T(1,128)S(1)} all-to-all(f32[32,1,128]{2,1,0:T(1,128)S(1)} %bitcast.17), channel_id=1, replica_groups=mesh['blk'=8,'col'=4] {'blk','col'}, dimensions={0} | all-to-all | bytes 32768 | tf_op jit(solution)/shard_map/all_to_all | solution.py:218
  28.8 1.2 %shard_map.89 = (f32[2,128,128]{2,1,0:T(8,128)}, f32[1,1]{1,0:T(1,128)}) custom-call(f32[32,128]{1,0:T(8,128)S(1)} %bitcast.16, bf16[2,128,128]{2,1,0:T(8,128)(2,1)S(1)} %shard_map.86.rest_0_.held, f32[2,128,128]{2,1,0:T(8,128)S(1)} %get-tuple-element.14.resid, f32[2,128,128]{2,1,0:T(8,128)S(1)} %get-tuple-element.15.inverse), custom_call_target="tpu_custom_call" | custom-call | tf_op jit(solution)/shard_map/pallas_call | solution.py:219
  (1 shorter events, 0.0 us)
Async XLA Ops:
  0.6 6.5 %copy-start = (bf16[2,128,128]{2,1,0:T(8,128)(2,1)S(1)}, bf16[2,128,128]{2,1,0:T(8,128)(2,1)}, u32[]{:S(2)}) copy-start(bf16[2,128,128]{2,1,0:T(8,128)(2,1)} %own_in.1) | copy-start | bytes 196612
  1.5 7.2 %collective-permute-start = (bf16[2,128,128]{2,1,0:T(8,128)(2,1)S(1)}, bf16[2,128,128]{2,1,0:T(8,128)(2,1)S(1)}, u32[]{:S(2)}, u32[]{:S(2)}) collective-permute-start(bf16[2,128,128]{2,1,0:T(8,128)(2,1)S(1)} %shard_map.86.rest_0_.held), channel_id=1, source_target_pairs={{0,4},{4,0},{8,12},{12,8},{16,20},{20,16},{24,28},{28,24},{1,5},{5... | collective-permute-start | bytes 196616 | tf_op jit(solution)/shard_map/ppermute | solution.py:126
  4.5 6.4 %collective-permute-start.1 = (bf16[2,128,128]{2,1,0:T(8,128)(2,1)S(1)}, bf16[2,128,128]{2,1,0:T(8,128)(2,1)S(1)}, u32[]{:S(2)}, u32[]{:S(2)}) collective-permute-start(bf16[2,128,128]{2,1,0:T(8,128)(2,1)S(1)} %shard_map.86.rest_0_.held), channel_id=1, source_target_pairs={{0,16},{4,20},{8,24},{12,28},{16,0},{20,4},{24,8},{28,12},{1,17},{... | collective-permute-start | bytes 196616 | tf_op jit(solution)/shard_map/ppermute | solution.py:126
  7.1 4.7 %collective-permute-start.2 = (bf16[2,128,128]{2,1,0:T(8,128)(2,1)S(1)}, bf16[2,128,128]{2,1,0:T(8,128)(2,1)S(1)}, u32[]{:S(2)}, u32[]{:S(2)}) collective-permute-start(bf16[2,128,128]{2,1,0:T(8,128)(2,1)S(1)} %copy-done), channel_id=1, source_target_pairs={{0,1},{1,0},{2,3},{3,2},{4,5},{5,4},{6,7},{7,6},{8,9},{9,8},{10,11... | collective-permute-start | bytes 196616 | tf_op jit(solution)/shard_map/ppermute | solution.py:126
  7.1 5.7 %collective-permute-start.3 = (bf16[2,128,128]{2,1,0:T(8,128)(2,1)S(1)}, bf16[2,128,128]{2,1,0:T(8,128)(2,1)S(1)}, u32[]{:S(2)}, u32[]{:S(2)}) collective-permute-start(bf16[2,128,128]{2,1,0:T(8,128)(2,1)S(1)} %copy-done), channel_id=1, source_target_pairs={{0,3},{1,2},{2,1},{3,0},{4,7},{5,6},{6,5},{7,4},{8,11},{9,10},{10,... | collective-permute-start | bytes 196616 | tf_op jit(solution)/shard_map/ppermute | solution.py:126
  8.8 8.4 %collective-permute-start.8 = (bf16[4,128,128]{2,1,0:T(8,128)(2,1)S(1)}, bf16[4,128,128]{2,1,0:T(8,128)(2,1)S(1)}, u32[]{:S(2)}, u32[]{:S(2)}) collective-permute-start(bf16[4,128,128]{2,1,0:T(8,128)(2,1)S(1)} %pad_maximum_fusion), channel_id=1, source_target_pairs={{0,8},{4,12},{8,0},{12,4},{16,24},{20,28},{24,16},{28,20},{1,9},{5... | collective-permute-start | bytes 393224 | tf_op jit(solution)/shard_map/ppermute | solution.py:126
  10.4 4.3 %collective-permute-start.4 = (bf16[2,128,128]{2,1,0:T(8,128)(2,1)S(1)}, bf16[2,128,128]{2,1,0:T(8,128)(2,1)S(1)}, u32[]{:S(2)}, u32[]{:S(2)}) collective-permute-start(bf16[2,128,128]{2,1,0:T(8,128)(2,1)S(1)} %copy-done), channel_id=1, source_target_pairs={{0,2},{1,3},{2,0},{3,1},{4,6},{5,7},{6,4},{7,5},{8,10},{9,11},{10,... | collective-permute-start | bytes 196616 | tf_op jit(solution)/shard_map/ppermute | solution.py:126
  10.9 5.4 %collective-permute-start.5 = (bf16[2,128,128]{2,1,0:T(8,128)(2,1)S(1)}, bf16[2,128,128]{2,1,0:T(8,128)(2,1)S(1)}, u32[]{:S(2)}, u32[]{:S(2)}) collective-permute-start(bf16[2,128,128]{2,1,0:T(8,128)(2,1)S(1)} %collective-permute-done.1.rest_2_), channel_id=1, source_target_pairs={{0,12},{4,8},{8,4},{12,0},{16,28},{20,24},{24,20},{28,16},{1,13},{... | collective-permute-start | bytes 196616 | tf_op jit(solution)/shard_map/ppermute | solution.py:126
  11.9 5.0 %collective-permute-start.6 = (bf16[2,128,128]{2,1,0:T(8,128)(2,1)S(1)}, bf16[2,128,128]{2,1,0:T(8,128)(2,1)S(1)}, u32[]{:S(2)}, u32[]{:S(2)}) collective-permute-start(bf16[2,128,128]{2,1,0:T(8,128)(2,1)S(1)} %collective-permute-done.1.rest_2_), channel_id=1, source_target_pairs={{0,4},{4,0},{8,12},{12,8},{16,20},{20,16},{24,28},{28,24},{1,5},{5... | collective-permute-start | bytes 196616 | tf_op jit(solution)/shard_map/ppermute | solution.py:126
  12.9 4.3 %collective-permute-start.7 = (bf16[2,128,128]{2,1,0:T(8,128)(2,1)S(1)}, bf16[2,128,128]{2,1,0:T(8,128)(2,1)S(1)}, u32[]{:S(2)}, u32[]{:S(2)}) collective-permute-start(bf16[2,128,128]{2,1,0:T(8,128)(2,1)S(1)} %collective-permute-done.1.rest_2_), channel_id=1, source_target_pairs={{0,8},{4,12},{8,0},{12,4},{16,24},{20,28},{24,16},{28,20},{1,9},{5... | collective-permute-start | bytes 196616 | tf_op jit(solution)/shard_map/ppermute | solution.py:126
